TPU v7x, 32 devices: a whole 2x2x4 slice. The times are simulated.
32 devices in a mesh: section: 2 (over y), batch: 16 (over z, x, core).
Axes of the slice: x: 2, y: 2, z: 4, core: 2. Of those that a mesh axis runs over, the one named last changes fastest.
Arguments:
- tokens: bfloat16 [2, 2048, 1024], P(None, 'batch'), may hold values from -13.5 to 13.5
- lengths: int32 [2, 16], P(None, 'batch'), may hold values from 26 to 128, as said below
- norm_gain: bfloat16 [2, 1024], P('section', 'batch'), may hold values from 0.5 to 1.5
- norm_bias: bfloat16 [2, 1024], P('section', 'batch'), may hold values from -1.1953125 to 1.1953125
- joint_weight: bfloat16 [2, 1024, 3072], P('section', 'batch'), may hold values from -0.1875 to 0.1875
- joint_bias: bfloat16 [2, 2048], P('section', 'batch'), may hold values from -1.1953125 to 1.1953125
- output_weight: bfloat16 [2, 1024, 1024], P('section', 'batch'), may hold values from -0.1875 to 0.1875
- output_bias: bfloat16 [2, 1024], P('section', 'batch'), may hold values from -1.1953125 to 1.1953125
- sandwich_gain: bfloat16 [2, 1024], P('section', 'batch'), may hold values from 0.5 to 1.5
- sandwich_bias: bfloat16 [2, 1024], P('section', 'batch'), may hold values from -1.1953125 to 1.1953125
- second_gain: bfloat16 [2, 1024], P('section', 'batch'), may hold values from 0.5 to 1.5
- second_bias: bfloat16 [2, 1024], P('section', 'batch'), may hold values from -1.1953125 to 1.1953125
- expand_weight: bfloat16 [2, 1024, 4096], P('section', 'batch'), may hold values from -0.1875 to 0.1875
- expand_bias: bfloat16 [2, 4096], P('section', 'batch'), may hold values from -1.1953125 to 1.1953125
- reduce_weight: bfloat16 [2, 4096, 1024], P('section', 'batch'), may hold values from -0.09375 to 0.09375
- reduce_bias: bfloat16 [2, 1024], P('section', 'batch'), may hold values from -1.1953125 to 1.1953125
- closing_gain: bfloat16 [2, 1024], P('section', 'batch'), may hold values from 0.5 to 1.5
- closing_bias: bfloat16 [2, 1024], P('section', 'batch'), may hold values from -1.1953125 to 1.1953125
- cotangent: bfloat16 [2, 2048, 1024], P(None, 'batch'), may hold values from -6 to 6
Outputs:
- section_out: bfloat16 [2, 2, 2048, 1024], P('section', None, 'batch')
- section_grad: float32 [2, 2, 2048, 1024], P('section', None, 'batch')
- magnitudes: float32 [2, 3], P('section')
- grad_norm_gain: float32 [2, 1024], P('section', 'batch')
- grad_norm_bias: float32 [2, 1024], P('section', 'batch')
- grad_joint_weight: float32 [2, 1024, 3072], P('section', 'batch')
- grad_joint_bias: float32 [2, 2048], P('section', 'batch')
- grad_output_weight: float32 [2, 1024, 1024], P('section', 'batch')
- grad_output_bias: float32 [2, 1024], P('section', 'batch')
- grad_sandwich_gain: float32 [2, 1024], P('section', 'batch')
- grad_sandwich_bias: float32 [2, 1024], P('section', 'batch')
- grad_second_gain: float32 [2, 1024], P('section', 'batch')
- grad_second_bias: float32 [2, 1024], P('section', 'batch')
- grad_expand_weight: float32 [2, 1024, 4096], P('section', 'batch')
- grad_expand_bias: float32 [2, 4096], P('section', 'batch')
- grad_reduce_weight: float32 [2, 4096, 1024], P('section', 'batch')
- grad_reduce_bias: float32 [2, 1024], P('section', 'batch')
- grad_closing_gain: float32 [2, 1024], P('section', 'batch')
- grad_closing_bias: float32 [2, 1024], P('section', 'batch')
Inputs may be any that keep to these rules, and one draw needn't show every extreme that they name: lengths[m, s] is the number of used slots of sequence row s in micro-batch m; later slots are padding.
All inputs are finite; a program needn't handle non-finite values.
Results may differ from a plain program's by a relative error of at most 0.014.
Values may be sent and summed in bfloat16 or wider, within the bound.
A program may use at most 256 MiB of HBM per device.

v0:
```python
import math

import jax
import jax.numpy as jnp
from jax import lax
from jax.sharding import PartitionSpec as P

HEADS = 16
HEAD_DIM = 64


epsilon = 1e-05
relax_scale = 32.0
masked_value = -1000000000.0


def passed_along(block, axis, distance):
    devices = range(lax.axis_size(axis))
    route = [(i - distance, i) for i in devices if i - distance in devices]
    return lax.ppermute(block, axis, route)


def norm_layer(value, gain, shift):
    center = jnp.mean(value, axis=-1, keepdims=True)
    centered = value - center
    spread = jnp.mean(centered * centered, axis=-1, keepdims=True)
    return centered * lax.rsqrt(spread + epsilon) * gain + shift


def unpack(weights):
    return tuple((w if w.ndim == 2 else w.astype(jnp.float32) for w in weights))


def block_layout(row_count):
    block_size = min(row_count, 512)
    return (block_size, row_count // block_size)


def masked_scores(query_block, block_start, keys_all, length):
    scores = jnp.einsum("qhd,khd->hqk", query_block, keys_all, preferred_element_type=jnp.float32)
    score_shape = (query_block.shape[0], keys_all.shape[0])
    query_slot = block_start + lax.broadcasted_iota(jnp.int32, score_shape, 0)
    key_slot = lax.broadcasted_iota(jnp.int32, score_shape, 1)
    visible = (key_slot <= query_slot) & (key_slot < length)
    return jnp.where(visible[None], scores, masked_value)


def attention_fore(queries, keys_all, values_all, length):
    row_count = queries.shape[0]
    block_size, block_count = block_layout(row_count)
    starts = jnp.arange(block_count, dtype=jnp.int32) * block_size
    query_blocks = queries.reshape(block_count, block_size, HEADS, HEAD_DIM)

    def one_block(operand):
        query_block, block_start = operand
        scores = masked_scores(query_block, block_start, keys_all, length)
        row_max = jnp.max(scores, axis=-1, keepdims=True)
        exponent = jnp.exp(relax_scale * (scores - row_max))
        row_total = jnp.sum(exponent, axis=-1, keepdims=True)
        attn_probs = (exponent / row_total).astype(jnp.bfloat16)
        attended = jnp.einsum(
            "hqk,khd->qhd", attn_probs, values_all, preferred_element_type=jnp.float32
        )
        return (attended, row_max, row_total)

    attended, row_max, row_total = lax.map(one_block, (query_blocks, starts))
    return (attended.reshape(row_count, HEADS * HEAD_DIM), row_max, row_total)


def attention_back(queries, keys_all, values_all, grad_attended, row_max, row_total, length):
    row_count = queries.shape[0]
    block_size, block_count = block_layout(row_count)
    starts = jnp.arange(block_count, dtype=jnp.int32) * block_size
    query_blocks = queries.reshape(block_count, block_size, HEADS, HEAD_DIM)
    grad_blocks = grad_attended.reshape(block_count, block_size, HEADS, HEAD_DIM)

    def one_block(running, operand):
        query_block, grad_block, block_start, block_max, block_total = operand
        scores = masked_scores(query_block, block_start, keys_all, length)
        attn_probs = jnp.exp(relax_scale * (scores - block_max)) / block_total
        grad_probs = jnp.einsum(
            "qhd,khd->hqk", grad_block, values_all, preferred_element_type=jnp.float32
        )
        row_delta = jnp.sum(grad_probs * attn_probs, axis=-1, keepdims=True)
        grad_scores = (relax_scale * attn_probs * (grad_probs - row_delta)).astype(jnp.bfloat16)
        grad_query = jnp.einsum(
            "hqk,khd->qhd", grad_scores, keys_all, preferred_element_type=jnp.float32
        )
        grad_key = running[0] + jnp.einsum(
            "hqk,qhd->khd", grad_scores, query_block, preferred_element_type=jnp.float32
        )
        grad_value = running[1] + jnp.einsum(
            "hqk,qhd->khd",
            attn_probs.astype(jnp.bfloat16),
            grad_block,
            preferred_element_type=jnp.float32,
        )
        return ((grad_key, grad_value), grad_query)

    zero_grads = jnp.zeros((row_count, HEADS, HEAD_DIM), jnp.float32)
    (grad_key, grad_value), grad_query = lax.scan(
        one_block, (zero_grads, zero_grads), (query_blocks, grad_blocks, starts, row_max, row_total)
    )
    flat_shape = (row_count, HEADS * HEAD_DIM)
    return (
        grad_query.reshape(flat_shape),
        grad_key.reshape(flat_shape),
        grad_value.reshape(flat_shape),
    )


def layer_fore(hidden_in, weights, length, valid_row):
    (
        norm_gain,
        norm_bias,
        joint_weight,
        joint_bias,
        output_weight,
        output_bias,
        sandwich_gain,
        sandwich_bias,
        second_gain,
        second_bias,
        expand_weight,
        expand_bias,
        reduce_weight,
        reduce_bias,
        closing_gain,
        closing_bias,
    ) = unpack(weights)
    model_width = joint_weight.shape[0]
    row_count = hidden_in.shape[0]
    query_scale = 1.0 / (relax_scale * math.sqrt(HEAD_DIM))
    hidden = hidden_in.astype(jnp.float32)
    normed = norm_layer(hidden, norm_gain, norm_bias).astype(jnp.bfloat16)
    full_bias = jnp.concatenate(
        [joint_bias[:model_width], jnp.zeros((model_width,), jnp.float32), joint_bias[model_width:]]
    )
    mixed = jnp.dot(normed, joint_weight, preferred_element_type=jnp.float32) + full_bias
    head_shape = (row_count, HEADS, HEAD_DIM)
    queries = (mixed[:, :model_width] * query_scale).astype(jnp.bfloat16).reshape(head_shape)
    keys_all = mixed[:, model_width : 2 * model_width].astype(jnp.bfloat16).reshape(head_shape)
    values_all = mixed[:, 2 * model_width :].astype(jnp.bfloat16).reshape(head_shape)
    attended, row_max, row_total = attention_fore(queries, keys_all, values_all, length)
    attended = attended.astype(jnp.bfloat16)
    branch = jnp.dot(attended, output_weight, preferred_element_type=jnp.float32) + output_bias
    middle = hidden + norm_layer(branch, sandwich_gain, sandwich_bias)
    inner = norm_layer(middle, second_gain, second_bias).astype(jnp.bfloat16)
    before = jnp.dot(inner, expand_weight, preferred_element_type=jnp.float32) + expand_bias
    active = jax.nn.gelu(before).astype(jnp.bfloat16)
    feed = jnp.dot(active, reduce_weight, preferred_element_type=jnp.float32) + reduce_bias
    result = middle + norm_layer(feed, closing_gain, closing_bias)
    factor = valid_row[:, None]
    squares = jnp.stack(
        [
            jnp.sum(branch * branch * factor),
            jnp.sum(feed * feed * factor),
            jnp.sum(result * result * factor),
        ]
    )
    kept_state = (
        hidden_in,
        normed,
        queries,
        keys_all,
        values_all,
        row_max,
        row_total,
        attended,
        branch,
        middle,
        inner,
        before,
        active,
        feed,
    )
    return (result.astype(jnp.bfloat16), squares, kept_state)


def blank_fore(operand, hidden_width):
    source = operand[0]
    row_count = source.shape[0]
    model_width = source.shape[1]
    block_size, block_count = block_layout(row_count)
    flat_low = jnp.zeros((row_count, model_width), jnp.bfloat16)
    flat_high = jnp.zeros((row_count, model_width), jnp.float32)
    head_low = jnp.zeros((row_count, HEADS, HEAD_DIM), jnp.bfloat16)
    stats_zero = jnp.zeros((block_count, HEADS, block_size, 1), jnp.float32)
    kept_state = (
        flat_low,
        flat_low,
        head_low,
        head_low,
        head_low,
        stats_zero,
        stats_zero,
        flat_low,
        flat_high,
        flat_high,
        flat_low,
        jnp.zeros((row_count, hidden_width), jnp.float32),
        jnp.zeros((row_count, hidden_width), jnp.bfloat16),
        flat_high,
    )
    return (flat_low, jnp.zeros((3,), jnp.float32), kept_state)


def back_feed(grad_seed, kept_state, weights):
    (
        hidden_in,
        normed,
        queries,
        keys_all,
        values_all,
        row_max,
        row_total,
        attended,
        branch,
        middle,
        inner,
        before,
        active,
        feed,
    ) = kept_state
    (
        norm_gain,
        norm_bias,
        joint_weight,
        joint_bias,
        output_weight,
        output_bias,
        sandwich_gain,
        sandwich_bias,
        second_gain,
        second_bias,
        expand_weight,
        expand_bias,
        reduce_weight,
        reduce_bias,
        closing_gain,
        closing_bias,
    ) = unpack(weights)
    norm_pull = jax.vjp(norm_layer, feed, closing_gain, closing_bias)[1]
    grad_feed, grad_closing_gain, grad_closing_bias = norm_pull(grad_seed)
    grad_feed = grad_feed.astype(jnp.bfloat16)
    grad_reduce_weight = jnp.einsum(
        "tf,td->fd", active, grad_feed, preferred_element_type=jnp.float32
    )
    grad_reduce_bias = jnp.sum(grad_feed.astype(jnp.float32), axis=0)
    grad_active = jnp.einsum(
        "td,fd->tf", grad_feed, reduce_weight, preferred_element_type=jnp.float32
    )
    gelu_pull = jax.vjp(jax.nn.gelu, before)[1]
    grad_before = gelu_pull(grad_active)[0].astype(jnp.bfloat16)
    grad_expand_weight = jnp.einsum(
        "td,tf->df", inner, grad_before, preferred_element_type=jnp.float32
    )
    grad_expand_bias = jnp.sum(grad_before.astype(jnp.float32), axis=0)
    grad_inner = jnp.einsum(
        "tf,df->td", grad_before, expand_weight, preferred_element_type=jnp.float32
    )
    norm_pull = jax.vjp(norm_layer, middle, second_gain, second_bias)[1]
    grad_middle, grad_second_gain, grad_second_bias = norm_pull(grad_inner)
    grad_middle = grad_middle + grad_seed
    return (
        grad_middle,
        (
            grad_second_gain,
            grad_second_bias,
            grad_expand_weight,
            grad_expand_bias,
            grad_reduce_weight,
            grad_reduce_bias,
            grad_closing_gain,
            grad_closing_bias,
        ),
    )


def back_attention(grad_middle, kept_state, weights, length):
    (
        hidden_in,
        normed,
        queries,
        keys_all,
        values_all,
        row_max,
        row_total,
        attended,
        branch,
        middle,
        inner,
        before,
        active,
        feed,
    ) = kept_state
    (
        norm_gain,
        norm_bias,
        joint_weight,
        joint_bias,
        output_weight,
        output_bias,
        sandwich_gain,
        sandwich_bias,
        second_gain,
        second_bias,
        expand_weight,
        expand_bias,
        reduce_weight,
        reduce_bias,
        closing_gain,
        closing_bias,
    ) = unpack(weights)
    model_width = joint_weight.shape[0]
    row_count = hidden_in.shape[0]
    query_scale = 1.0 / (relax_scale * math.sqrt(HEAD_DIM))
    norm_pull = jax.vjp(norm_layer, branch, sandwich_gain, sandwich_bias)[1]
    grad_branch, grad_sandwich_gain, grad_sandwich_bias = norm_pull(grad_middle)
    grad_branch = grad_branch.astype(jnp.bfloat16)
    grad_output_weight = jnp.einsum(
        "te,td->ed", attended, grad_branch, preferred_element_type=jnp.float32
    )
    grad_output_bias = jnp.sum(grad_branch.astype(jnp.float32), axis=0)
    grad_attended = jnp.einsum(
        "td,ed->te", grad_branch, output_weight, preferred_element_type=jnp.float32
    )
    grad_attended = grad_attended.astype(jnp.bfloat16).reshape(row_count, HEADS, HEAD_DIM)
    grad_query, grad_key, grad_value = attention_back(
        queries, keys_all, values_all, grad_attended, row_max, row_total, length
    )
    grad_mixed = jnp.concatenate([grad_query * query_scale, grad_key, grad_value], axis=1).astype(
        jnp.bfloat16
    )
    grad_joint_weight = jnp.einsum(
        "td,te->de", normed, grad_mixed, preferred_element_type=jnp.float32
    )
    mixed_float = grad_mixed.astype(jnp.float32)
    grad_joint_bias = jnp.concatenate(
        [
            jnp.sum(mixed_float[:, :model_width], axis=0),
            jnp.sum(mixed_float[:, 2 * model_width :], axis=0),
        ]
    )
    grad_normed = jnp.einsum(
        "te,de->td", grad_mixed, joint_weight, preferred_element_type=jnp.float32
    )
    norm_pull = jax.vjp(norm_layer, hidden_in.astype(jnp.float32), norm_gain, norm_bias)[1]
    grad_hidden, grad_norm_gain, grad_norm_bias = norm_pull(grad_normed)
    grad_in = grad_middle + grad_hidden
    return (
        grad_in,
        (
            grad_norm_gain,
            grad_norm_bias,
            grad_joint_weight,
            grad_joint_bias,
            grad_output_weight,
            grad_output_bias,
            grad_sandwich_gain,
            grad_sandwich_bias,
        ),
    )


def layer_back(grad_seed, kept_state, weights, length):
    grad_middle, feed_part = back_feed(grad_seed, kept_state, weights)
    grad_in, attention_part = back_attention(grad_middle, kept_state, weights, length)
    return (grad_in, tuple(attention_part) + tuple(feed_part))


def local(
    tokens,
    lengths,
    norm_gain,
    norm_bias,
    joint_weight,
    joint_bias,
    output_weight,
    output_bias,
    sandwich_gain,
    sandwich_bias,
    second_gain,
    second_bias,
    expand_weight,
    expand_bias,
    reduce_weight,
    reduce_bias,
    closing_gain,
    closing_bias,
    cotangent,
):
    section_index = lax.axis_index("section")
    micro_count = tokens.shape[0]
    row_count = tokens.shape[1]
    model_width = tokens.shape[2]
    gathered = (
        lax.all_gather(norm_gain, "batch", axis=1, tiled=True),
        lax.all_gather(norm_bias, "batch", axis=1, tiled=True),
        lax.all_gather(joint_weight, "batch", axis=1, tiled=True),
        lax.all_gather(joint_bias, "batch", axis=1, tiled=True),
        lax.all_gather(output_weight, "batch", axis=1, tiled=True),
        lax.all_gather(output_bias, "batch", axis=1, tiled=True),
        lax.all_gather(sandwich_gain, "batch", axis=1, tiled=True),
        lax.all_gather(sandwich_bias, "batch", axis=1, tiled=True),
        lax.all_gather(second_gain, "batch", axis=1, tiled=True),
        lax.all_gather(second_bias, "batch", axis=1, tiled=True),
        lax.all_gather(expand_weight, "batch", axis=1, tiled=True),
        lax.all_gather(expand_bias, "batch", axis=1, tiled=True),
        lax.all_gather(reduce_weight, "batch", axis=1, tiled=True),
        lax.all_gather(reduce_bias, "batch", axis=1, tiled=True),
        lax.all_gather(closing_gain, "batch", axis=1, tiled=True),
        lax.all_gather(closing_bias, "batch", axis=1, tiled=True),
    )
    weights = tuple((x[0] for x in gathered))
    hidden_width = weights[10].shape[1]
    positions = lax.broadcasted_iota(jnp.int32, (micro_count, row_count), 1)
    valid_mask = (positions < lengths).astype(jnp.float32)

    def run_fore(operand):
        return layer_fore(operand[0], weights, operand[1], operand[2])

    def skip_fore(operand):
        return blank_fore(operand, hidden_width)

    incoming = jnp.zeros((row_count, model_width), jnp.bfloat16)
    results = []
    kept_list = []
    square_sum = jnp.zeros((3,), jnp.float32)
    for clock_tick in range(micro_count + 1):
        position = clock_tick - section_index
        active_now = (position >= 0) & (position < micro_count)
        micro_index = jnp.clip(position, 0, micro_count - 1)
        own_rows = lax.dynamic_index_in_dim(tokens, micro_index, 0, keepdims=False)
        source = jnp.where(section_index == 0, own_rows, incoming)
        length = lax.dynamic_index_in_dim(lengths, micro_index, 0, keepdims=False)[0]
        valid_row = lax.dynamic_index_in_dim(valid_mask, micro_index, 0, keepdims=False)
        operand = (source, length, valid_row)
        result, squares, kept_state = lax.cond(active_now, run_fore, skip_fore, operand)
        results.append(result)
        kept_list.append(kept_state)
        square_sum = square_sum + squares
        if clock_tick < micro_count:
            incoming = passed_along(result, "section", 1)
    result_stack = jnp.stack(results)
    section_out = lax.dynamic_slice_in_dim(result_stack, section_index, micro_count, 0)[None]
    kept_stack = jax.tree.map(lambda *x: jnp.stack(x), *kept_list)
    regathered = (
        lax.all_gather(norm_gain, "batch", axis=1, tiled=True),
        lax.all_gather(norm_bias, "batch", axis=1, tiled=True),
        lax.all_gather(joint_weight, "batch", axis=1, tiled=True),
        lax.all_gather(joint_bias, "batch", axis=1, tiled=True),
        lax.all_gather(output_weight, "batch", axis=1, tiled=True),
        lax.all_gather(output_bias, "batch", axis=1, tiled=True),
        lax.all_gather(sandwich_gain, "batch", axis=1, tiled=True),
        lax.all_gather(sandwich_bias, "batch", axis=1, tiled=True),
        lax.all_gather(second_gain, "batch", axis=1, tiled=True),
        lax.all_gather(second_bias, "batch", axis=1, tiled=True),
        lax.all_gather(expand_weight, "batch", axis=1, tiled=True),
        lax.all_gather(expand_bias, "batch", axis=1, tiled=True),
        lax.all_gather(reduce_weight, "batch", axis=1, tiled=True),
        lax.all_gather(reduce_bias, "batch", axis=1, tiled=True),
        lax.all_gather(closing_gain, "batch", axis=1, tiled=True),
        lax.all_gather(closing_bias, "batch", axis=1, tiled=True),
    )
    weights_back = tuple((x[0] for x in regathered))

    def run_back(operand):
        grad_in, layer_grads = layer_back(operand[0], operand[1], weights_back, operand[2])
        return (grad_in, jax.tree.map(jnp.add, operand[3], layer_grads))

    def skip_back(operand):
        return (jnp.zeros_like(operand[0]), operand[3])

    running = tuple((jnp.zeros(x.shape, jnp.float32) for x in weights_back))
    incoming_grad = jnp.zeros((row_count, model_width), jnp.bfloat16)
    grad_list = []
    for clock_tick in range(micro_count + 1):
        position = clock_tick - 1 + section_index
        active_now = (position >= 0) & (position < micro_count)
        micro_index = jnp.clip(position, 0, micro_count - 1)
        saved_slot = micro_index + section_index
        kept_state = jax.tree.map(
            lambda x: lax.dynamic_index_in_dim(x, saved_slot, 0, keepdims=False), kept_stack
        )
        length = lax.dynamic_index_in_dim(lengths, micro_index, 0, keepdims=False)[0]
        valid_row = lax.dynamic_index_in_dim(valid_mask, micro_index, 0, keepdims=False)
        own_seed = lax.dynamic_index_in_dim(cotangent, micro_index, 0, keepdims=False).astype(
            jnp.float32
        )
        own_seed = own_seed * valid_row[:, None]
        grad_seed = jnp.where(section_index == 1, own_seed, incoming_grad.astype(jnp.float32))
        grad_in, running = lax.cond(
            active_now, run_back, skip_back, (grad_seed, kept_state, length, running)
        )
        grad_list.append(grad_in)
        if clock_tick < micro_count:
            incoming_grad = passed_along(grad_in.astype(jnp.bfloat16), "section", -1)
    grad_stack = jnp.stack(grad_list)
    section_grad = lax.dynamic_slice_in_dim(grad_stack, 1 - section_index, micro_count, 0)[None]
    lifted = [x[None] for x in running]
    grads_out = tuple(
        (
            lax.psum_scatter(lifted[0], "batch", scatter_dimension=1, tiled=True),
            lax.psum_scatter(lifted[1], "batch", scatter_dimension=1, tiled=True),
            lax.psum_scatter(lifted[2], "batch", scatter_dimension=1, tiled=True),
            lax.psum_scatter(lifted[3], "batch", scatter_dimension=1, tiled=True),
            lax.psum_scatter(lifted[4], "batch", scatter_dimension=1, tiled=True),
            lax.psum_scatter(lifted[5], "batch", scatter_dimension=1, tiled=True),
            lax.psum_scatter(lifted[6], "batch", scatter_dimension=1, tiled=True),
            lax.psum_scatter(lifted[7], "batch", scatter_dimension=1, tiled=True),
            lax.psum_scatter(lifted[8], "batch", scatter_dimension=1, tiled=True),
            lax.psum_scatter(lifted[9], "batch", scatter_dimension=1, tiled=True),
            lax.psum_scatter(lifted[10], "batch", scatter_dimension=1, tiled=True),
            lax.psum_scatter(lifted[11], "batch", scatter_dimension=1, tiled=True),
            lax.psum_scatter(lifted[12], "batch", scatter_dimension=1, tiled=True),
            lax.psum_scatter(lifted[13], "batch", scatter_dimension=1, tiled=True),
            lax.psum_scatter(lifted[14], "batch", scatter_dimension=1, tiled=True),
            lax.psum_scatter(lifted[15], "batch", scatter_dimension=1, tiled=True),
        )
    )
    token_count = jnp.sum(lengths).astype(jnp.float32)
    square_all, count_all = lax.psum((square_sum, token_count), "batch")
    magnitudes = jnp.sqrt(square_all / (count_all * model_width))[None]
    return (
        section_out,
        section_grad,
        magnitudes,
        grads_out[0],
        grads_out[1],
        grads_out[2],
        grads_out[3],
        grads_out[4],
        grads_out[5],
        grads_out[6],
        grads_out[7],
        grads_out[8],
        grads_out[9],
        grads_out[10],
        grads_out[11],
        grads_out[12],
        grads_out[13],
        grads_out[14],
        grads_out[15],
    )


def solution(mesh):
    placed = (
        P(None, "batch", None),
        P(None, "batch"),
        P("section", "batch"),
        P("section", "batch"),
        P("section", "batch", None),
        P("section", "batch"),
        P("section", "batch", None),
        P("section", "batch"),
        P("section", "batch"),
        P("section", "batch"),
        P("section", "batch"),
        P("section", "batch"),
        P("section", "batch", None),
        P("section", "batch"),
        P("section", "batch", None),
        P("section", "batch"),
        P("section", "batch"),
        P("section", "batch"),
        P(None, "batch", None),
    )
    return jax.shard_map(
        local,
        mesh=mesh,
        in_specs=placed,
        out_specs=(
            P("section", None, "batch", None),
            P("section", None, "batch", None),
            P("section", None),
            P("section", "batch"),
            P("section", "batch"),
            P("section", "batch", None),
            P("section", "batch"),
            P("section", "batch", None),
            P("section", "batch"),
            P("section", "batch"),
            P("section", "batch"),
            P("section", "batch"),
            P("section", "batch"),
            P("section", "batch", None),
            P("section", "batch"),
            P("section", "batch", None),
            P("section", "batch"),
            P("section", "batch"),
            P("section", "batch"),
        ),
        check_vma=False,
    )
```

profile of v0, /device:TPU:0, one launch (start us, length us, event | category | flops | bytes accessed | tf_op | source)
XLA Modules:
  0.0 2069.0 jit_solution(7243307043825155160)
XLA Ops:
  61.4 60.7 %all-reduce.11 = (bf16[1024]{0:T(1024)(128)(2,1)S(1)}, bf16[1024]{0:T(1024)(128)(2,1)}, bf16[1024]{0:T(1024)(128)(2,1)}, bf16[1024]{0:T(1024)(128)(2,1)}, bf16[1...) all-reduce(bf16[1024]{0:T(1024)(128)(2,1)S(1)} %dynamic-update-slic, ...), channel_id=1, replica_groups=mesh['section'=2,'batch'=16] {'batch'}, use_global_device_ids=true, to_apply=%add | all-reduce | flops 10240 | bytes 40960 | tf_op jit(solution)/shard_map/squeeze | solution.py:415
  123.3 70.5 %all-gather.9.cloned.1.call-done = bf16[1,1024,4096]{2,1,0:T(8,128)(2,1)} async-done(((bf16[1,64,4096]{2,1,0:T(8,128)(2,1)}), bf16[1,1024,4096]{2,1,0:T(8,128)(2,1)}) %all-gather.9.cloned.1.call-update) | async-done | bytes 8388624 | tf_op jit(solution)/shard_map/all_gather | solution.py:408
  193.8 75.2 %all-gather.11.cloned.1.call-done = bf16[1,4096,1024]{2,1,0:T(8,128)(2,1)} async-done(((bf16[1,256,1024]{2,1,0:T(8,128)(2,1)}), bf16[1,4096,1024]{2,1,0:T(8,128)(2,1)}) %all-gather.11.cloned.1.call-update) | async-done | bytes 8388624 | tf_op jit(solution)/shard_map/all_gather | solution.py:410
  269.1 42.7 %conditional.6 = (bf16[128,1024]{1,0:T(8,128)(2,1)}, f32[3]{0:T(128)}, bf16[1,128,1024]{2,1,0:T(8,128)(2,1)S(1)}, bf16[1,128,1024]{2,1,0:T(8,128)(2,1)S(1)}, bf1...) conditional(s32[]{:T(128)} %convert_element_type.751, ...), branch_computations={%region_0.1_spmd, %region_1.15_spmd} | conditional | flops 3310142208 | bytes 101895072 | solution.py:439
  328.4 60.4 %conditional.7 = (bf16[128,1024]{1,0:T(8,128)(2,1)}, f32[3]{0:T(128)}, bf16[1,128,1024]{2,1,0:T(8,128)(2,1)}, bf16[1,128,1024]{2,1,0:T(8,128)(2,1)}, bf16[1,128,...) conditional(s32[]{:T(128)} %convert_element_type.753, ...), branch_computations={%region_15.16_spmd, %region_16.30_spmd} | conditional | flops 3310142208 | bytes 81368048 | solution.py:439
  448.7 38.1 %conditional.9 = (f32[128,1024]{1,0:T(8,128)S(1)}, f32[1024]{0:T(1024)S(1)}, f32[1024]{0:T(1024)S(1)}, f32[1024,3072]{1,0:T(8,128)}, f32[2048]{0:T(1024)S(1)}, /...) conditional(s32[]{:T(128)} %convert_element_type.755, ...), branch_computations={%region_45.46_spmd, %region_46.77_spmd} | conditional | flops 6646553600 | bytes 195791520 | solution.py:493
  489.1 90.6 %collective-permute-done.2 = bf16[128,1024]{1,0:T(8,128)(2,1)S(1)} collective-permute-done((bf16[128,1024]{1,0:T(8,128)(2,1)S(1)}, bf16[128,1024]{1,0:T(8,128)(2,1)S(1)}, u32[]{:S(2)}, u32[]{:S(2)}) %collective-permute-start.2) | collective-permute-done | bytes 262176 | tf_op jit(solution)/shard_map/ppermute | solution.py:20
  579.7 92.8 %conditional.10 = (f32[128,1024]{1,0:T(8,128)}, f32[1024]{0:T(1024)}, f32[1024]{0:T(1024)}, f32[1024,3072]{1,0:T(8,128)}, f32[2048]{0:T(1024)}, /*index=5*/f32[1...) conditional(s32[]{:T(128)} %convert_element_type.756, ...), branch_computations={%region_77.78_spmd, %region_78.109_spmd} | conditional | flops 6658366464 | bytes 224880608 | solution.py:493
  682.9 92.1 %conditional.11 = (f32[1024]{0:T(1024)}, f32[1024]{0:T(1024)}, f32[1024,3072]{1,0:T(8,128)}, f32[2048]{0:T(1024)}, f32[1024,1024]{1,0:T(8,128)}, /*index=5*/f32[...) conditional(s32[]{:T(128)} %convert_element_type.759, ...), branch_computations={%region_109.110_spmd, %region_110.141_spmd} | conditional | flops 6658366464 | bytes 224881152 | solution.py:493
  833.4 55.4 %reduce-scatter.51.cloned.1.call-done = f32[64,1]{1,0:T(8,128)} async-done(((f32[1024,1]{1,0:T(8,128)}), f32[64,1]{1,0:T(8,128)}) %reduce-scatter.51.cloned.1.call-update) | async-done | bytes 272
  890.2 57.0 %reduce-scatter.55.cloned.1.call-done = f32[64,1]{1,0:T(8,128)} async-done(((f32[1024,1]{1,0:T(8,128)}), f32[64,1]{1,0:T(8,128)}) %reduce-scatter.55.cloned.1.call-update) | async-done | bytes 272
  948.5 57.5 %reduce-scatter.57.cloned.1.call-done = f32[64,1]{1,0:T(8,128)} async-done(((f32[1024,1]{1,0:T(8,128)}), f32[64,1]{1,0:T(8,128)}) %reduce-scatter.57.cloned.1.call-update) | async-done | bytes 272
  1007.4 57.0 %reduce-scatter.59.cloned.1.call-done = f32[64,1]{1,0:T(8,128)} async-done(((f32[1024,1]{1,0:T(8,128)}), f32[64,1]{1,0:T(8,128)}) %reduce-scatter.59.cloned.1.call-update) | async-done | bytes 272
  1065.7 57.2 %reduce-scatter.61.cloned.1.call-done = f32[64,1]{1,0:T(8,128)} async-done(((f32[1024,1]{1,0:T(8,128)}), f32[64,1]{1,0:T(8,128)}) %reduce-scatter.61.cloned.1.call-update) | async-done | bytes 272
  1124.3 57.1 %reduce-scatter.63.cloned.1.call-done = f32[64,1]{1,0:T(8,128)} async-done(((f32[1024,1]{1,0:T(8,128)}), f32[64,1]{1,0:T(8,128)}) %reduce-scatter.63.cloned.1.call-update) | async-done | bytes 272
  1182.7 57.2 %reduce-scatter.67.cloned.1.call-done = f32[64,1]{1,0:T(8,128)} async-done(((f32[1024,1]{1,0:T(8,128)}), f32[64,1]{1,0:T(8,128)}) %reduce-scatter.67.cloned.1.call-update) | async-done | bytes 272
  1241.3 57.0 %reduce-scatter.69.cloned.1.call-done = f32[64,1]{1,0:T(8,128)} async-done(((f32[1024,1]{1,0:T(8,128)}), f32[64,1]{1,0:T(8,128)}) %reduce-scatter.69.cloned.1.call-update) | async-done | bytes 272
  1299.6 57.3 %reduce-scatter.71.cloned.1.call-done = f32[64,1]{1,0:T(8,128)} async-done(((f32[1024,1]{1,0:T(8,128)}), f32[64,1]{1,0:T(8,128)}) %reduce-scatter.71.cloned.1.call-update) | async-done | bytes 272
  1358.3 58.6 %reduce-scatter.53.cloned.1.call-done = f32[128,1]{1,0:T(8,128)} async-done(((f32[2048,1]{1,0:T(8,128)}), f32[128,1]{1,0:T(8,128)}) %reduce-scatter.53.cloned.1.call-update) | async-done | bytes 528
  1418.3 63.2 %reduce-scatter.65.cloned.1.call-done = f32[256,1]{1,0:T(8,128)} async-done(((f32[4096,1]{1,0:T(8,128)}), f32[256,1]{1,0:T(8,128)}) %reduce-scatter.65.cloned.1.call-update) | async-done | bytes 1040
  1483.1 74.4 %reduce-scatter.43.cloned.1.call-done = f32[1,64,1024]{2,1,0:T(8,128)} async-done(((f32[1,1024,1024]{2,1,0:T(8,128)}), f32[1,64,1024]{2,1,0:T(8,128)}) %reduce-scatter.43.cloned.1.call-update) | async-done | bytes 262160 | tf_op jit(solution)/shard_map/reduce_scatter | solution.py:508
  1557.5 138.9 %reduce-scatter.41.cloned.1.call-done = f32[1,64,3072]{2,1,0:T(8,128)} async-done(((f32[1,1024,3072]{2,1,0:T(8,128)}), f32[1,64,3072]{2,1,0:T(8,128)}) %reduce-scatter.41.cloned.1.call-update) | async-done | bytes 786448 | tf_op jit(solution)/shard_map/reduce_scatter | solution.py:506
  1696.3 182.9 %reduce-scatter.45.cloned.1.call-done = f32[1,64,4096]{2,1,0:T(8,128)} async-done(((f32[1,1024,4096]{2,1,0:T(8,128)}), f32[1,64,4096]{2,1,0:T(8,128)}) %reduce-scatter.45.cloned.1.call-update) | async-done | bytes 1048592 | tf_op jit(solution)/shard_map/reduce_scatter | solution.py:514
  1879.3 182.7 %reduce-scatter.47.cloned.1.call-done = f32[1,256,1024]{2,1,0:T(8,128)} async-done(((f32[1,4096,1024]{2,1,0:T(8,128)}), f32[1,256,1024]{2,1,0:T(8,128)}) %reduce-scatter.47.cloned.1.call-update) | async-done | bytes 1048592 | tf_op jit(solution)/shard_map/reduce_scatter | solution.py:516
  (675 shorter events, 540.6 us)
Async XLA Ops:
  7.2 116.1 %all-gather.7.cloned.1.call-start = ((), (), s32[]{:S(2)}) async-start(), calls=%async_computation.17 | async-start | bytes 2228224 | tf_op jit(solution)/shard_map/all_gather | solution.py:402
  7.9 115.4 %all-gather.5.cloned.1.call-start = ((), (), s32[]{:S(2)}) async-start(), calls=%async_computation.16 | async-start | bytes 6684672 | tf_op jit(solution)/shard_map/all_gather | solution.py:400
  8.7 185.2 %all-gather.9.cloned.1.call-start = ((), (), s32[]{:S(2)}) async-start(), calls=%async_computation.18 | async-start | bytes 8912896 | tf_op jit(solution)/shard_map/all_gather | solution.py:408
  9.4 259.6 %all-gather.11.cloned.1.call-start = ((), (), s32[]{:S(2)}) async-start(), calls=%async_computation.19 | async-start | bytes 8912896 | tf_op jit(solution)/shard_map/all_gather | solution.py:410
  10.0 822.1 %reduce-scatter.49.cloned.1.call-start = ((), (), s32[]{:S(2)}) async-start(), calls=%async_computation.24 | async-start | bytes 557056
  311.8 16.5 collective-permute-start
  388.8 25.7 %collective-permute-start.1 = (bf16[128,1024]{1,0:T(8,128)(2,1)}, bf16[128,1024]{1,0:T(8,128)(2,1)}, u32[]{:S(2)}, u32[]{:S(2)}) collective-permute-start(bf16[128,1024]{1,0:T(8,128)(2,1)} %get-tuple-element.2484), channel_id=1, source_target_pairs={{0,16},{1,17},{2,18},{3,19},{4,20},{5,21},{6,22},{7,23},{8,24},{9,... | collective-permute-start | bytes 786440 | tf_op jit(solution)/shard_map/ppermute | solution.py:20
  487.8 91.9 %collective-permute-start.2 = (bf16[128,1024]{1,0:T(8,128)(2,1)S(1)}, bf16[128,1024]{1,0:T(8,128)(2,1)S(1)}, u32[]{:S(2)}, u32[]{:S(2)}) collective-permute-start(bf16[128,1024]{1,0:T(8,128)(2,1)S(1)} %convert_element_type.757), channel_id=1, source_target_pairs={{16,0},{17,1},{18,2},{19,3},{20,4},{21,5},{22,6},{23,7},{24,8},{25... | collective-permute-start | bytes 786440 | tf_op jit(solution)/shard_map/ppermute | solution.py:20
  673.6 9.3 collective-permute-start.3
  776.8 112.0 %reduce-scatter.51.cloned.1.call-start = ((), (), s32[]{:S(2)}) async-start(), calls=%async_computation.25 | async-start | bytes 557056
  778.7 168.5 %reduce-scatter.55.cloned.1.call-start = ((), (), s32[]{:S(2)}) async-start(), calls=%async_computation.27 | async-start | bytes 557056
  780.5 225.5 %reduce-scatter.57.cloned.1.call-start = ((), (), s32[]{:S(2)}) async-start(), calls=%async_computation.28 | async-start | bytes 557056
  781.6 282.8 %reduce-scatter.59.cloned.1.call-start = ((), (), s32[]{:S(2)}) async-start(), calls=%async_computation.29 | async-start | bytes 557056
  782.7 340.2 %reduce-scatter.61.cloned.1.call-start = ((), (), s32[]{:S(2)}) async-start(), calls=%async_computation.30 | async-start | bytes 557056
  783.9 397.5 %reduce-scatter.63.cloned.1.call-start = ((), (), s32[]{:S(2)}) async-start(), calls=%async_computation.31 | async-start | bytes 557056
  785.0 454.9 %reduce-scatter.67.cloned.1.call-start = ((), (), s32[]{:S(2)}) async-start(), calls=%async_computation.33 | async-start | bytes 557056
  786.1 512.2 %reduce-scatter.69.cloned.1.call-start = ((), (), s32[]{:S(2)}) async-start(), calls=%async_computation.34 | async-start | bytes 557056
  787.2 569.7 %reduce-scatter.71.cloned.1.call-start = ((), (), s32[]{:S(2)}) async-start(), calls=%async_computation.35 | async-start | bytes 557056
  788.4 628.5 %reduce-scatter.53.cloned.1.call-start = ((), (), s32[]{:S(2)}) async-start(), calls=%async_computation.26 | async-start | bytes 1114112
  789.8 691.7 %reduce-scatter.65.cloned.1.call-start = ((), (), s32[]{:S(2)}) async-start(), calls=%async_computation.32 | async-start | bytes 2228224
  791.9 765.6 %reduce-scatter.43.cloned.1.call-start = ((), (), s32[]{:S(2)}) async-start(), calls=%async_computation.21 | async-start | bytes 4456448 | tf_op jit(solution)/shard_map/reduce_scatter | solution.py:508
  792.5 903.8 %reduce-scatter.41.cloned.1.call-start = ((), (), s32[]{:S(2)}) async-start(), calls=%async_computation.20 | async-start | bytes 13369344 | tf_op jit(solution)/shard_map/reduce_scatter | solution.py:506
  793.1 1086.2 %reduce-scatter.45.cloned.1.call-start = ((), (), s32[]{:S(2)}) async-start(), calls=%async_computation.22 | async-start | bytes 17825792 | tf_op jit(solution)/shard_map/reduce_scatter | solution.py:514
  793.8 1268.1 %reduce-scatter.47.cloned.1.call-start = ((), (), s32[]{:S(2)}) async-start(), calls=%async_computation.23 | async-start | bytes 17825792 | tf_op jit(solution)/shard_map/reduce_scatter | solution.py:516
  (127 other events, 1428.3 us)
Sparse Core Ops, SparseCore 0:
  10.2 44.1 all-gather.6
  56.7 61.3 all-gather.4
  120.2 73.5 all-gather.8
  195.8 73.1 all-gather.10
  777.0 53.1 reduce-scatter.48
  834.0 54.7 reduce-scatter.50
  892.4 54.7 reduce-scatter.54
  951.1 54.8 reduce-scatter.56
  1009.6 54.7 reduce-scatter.58
  1068.2 54.7 reduce-scatter.60
  1126.5 54.8 reduce-scatter.62
  1185.2 54.7 reduce-scatter.66
  1243.5 54.7 reduce-scatter.68
  1302.1 54.7 reduce-scatter.70
  1360.4 56.4 reduce-scatter.52
  1421.0 60.5 reduce-scatter.64
  1485.8 71.6 reduce-scatter.42
  1562.5 133.7 reduce-scatter.40
  1701.6 177.6 reduce-scatter.44
  1884.4 177.5 reduce-scatter.46
where the time goes:
time: 2080 us; the launch traced here: 2070 us
  waiting for transfers between devices  1460 us (70%)
  matrix products  170 us (8%)
  local copies, waits for them, and re-layouts  167 us (8%)
  blocking collectives  132 us (6%)
  other arithmetic  100 us (5%)
    unnamed x32, waiting for transfers between devices  640 us
    reduce_scatter x1, waiting for transfers between devices, local(): lax.psum_scatter(lifted[10], 'batch', scatter_dimension=1, tiled=True)  183 us
    reduce_scatter x1, waiting for transfers between devices, local(): lax.psum_scatter(lifted[12], 'batch', scatter_dimension=1, tiled=True)  183 us
    reduce_scatter x1, waiting for transfers between devices, local(): lax.psum_scatter(lifted[2], 'batch', scatter_dimension=1, tiled=True)  139 us
    ppermute x4, waiting for transfers between devices, passed_along(): return lax.ppermute(block, axis, route)  98.6 us
    unnamed x120, local copies, waits for them, and re-layouts  80.5 us
    all_gather x1, waiting for transfers between devices, local(): lax.all_gather(reduce_weight, 'batch', axis=1, tiled=True)  75.2 us
    reduce_scatter x1, waiting for transfers between devices, local(): lax.psum_scatter(lifted[4], 'batch', scatter_dimension=1, tiled=True)  74.4 us
  transfers between devices with their start and end apart: 24, of which 19 were waited for; matrix products, arithmetic and copies ran while one was open for 4% of the time, Pallas kernels for 0%

commit v1 on v0

v1 whole, which is shorter than its diff:
```python
import math

import jax
import jax.numpy as jnp
from jax import lax
from jax.sharding import PartitionSpec as P

HEADS = 16
HEAD_DIM = 64
EPSILON = 1e-05
RELAX = 32.0
MASKED = -1000000000.0
QUERY_SCALE = 1.0 / (RELAX * math.sqrt(HEAD_DIM))

BF = jnp.bfloat16
F32 = jnp.float32

VECTORS = (
    "norm_gain", "norm_bias", "joint_bias", "output_bias", "sandwich_gain", "sandwich_bias",
    "second_gain", "second_bias", "expand_bias", "reduce_bias", "closing_gain", "closing_bias",
)
MATRICES = ("joint_weight", "output_weight", "expand_weight", "reduce_weight")
ORDER = (
    "norm_gain", "norm_bias", "joint_weight", "joint_bias", "output_weight", "output_bias",
    "sandwich_gain", "sandwich_bias", "second_gain", "second_bias", "expand_weight", "expand_bias",
    "reduce_weight", "reduce_bias", "closing_gain", "closing_bias",
)


def dot(left, right, contract):
    return lax.dot_general(left, right, (contract, ((), ())), preferred_element_type=F32)


def norm_parts(value):
    center = jnp.mean(value, axis=-1, keepdims=True)
    centered = value - center
    rate = lax.rsqrt(jnp.mean(centered * centered, axis=-1, keepdims=True) + EPSILON)
    return centered * rate, rate


def norm_back(grad, normal, rate, gain):
    scaled = grad * gain
    first = jnp.mean(scaled, axis=-1, keepdims=True)
    second = jnp.mean(scaled * normal, axis=-1, keepdims=True)
    gain_grad = jnp.sum(grad * normal, axis=0)
    bias_grad = jnp.sum(grad, axis=0)
    return rate * (scaled - first - normal * second), gain_grad, bias_grad


def heads_of(flat, sequences):
    return flat.reshape(sequences, flat.shape[0] // sequences, HEADS, HEAD_DIM)


def layer_fore(hidden_in, w, lengths):
    sequences = lengths.shape[0]
    model = hidden_in.shape[1]
    hidden = hidden_in.astype(F32)
    n1, r1 = norm_parts(hidden)
    a = (n1 * w["norm_gain"] + w["norm_bias"]).astype(BF)
    mixed = dot(a, w["joint_weight"], ((1,), (0,)))
    q = ((mixed[:, :model] + w["joint_bias"][:model]) * QUERY_SCALE).astype(BF)
    k = mixed[:, model : 2 * model].astype(BF)
    v = (mixed[:, 2 * model :] + w["joint_bias"][model:]).astype(BF)
    qh, kh, vh = heads_of(q, sequences), heads_of(k, sequences), heads_of(v, sequences)
    scores = jnp.einsum("bqhd,bkhd->bhqk", qh, kh, preferred_element_type=F32)
    slots = scores.shape[-1]
    query_slot = lax.broadcasted_iota(jnp.int32, (sequences, slots, slots), 1)
    key_slot = lax.broadcasted_iota(jnp.int32, (sequences, slots, slots), 2)
    seen = (key_slot <= query_slot) & (key_slot < lengths[:, None, None])
    scores = jnp.where(seen[:, None], scores, MASKED)
    exponent = jnp.exp(RELAX * (scores - jnp.max(scores, axis=-1, keepdims=True)))
    probs = exponent / jnp.sum(exponent, axis=-1, keepdims=True)
    o = jnp.einsum("bhqk,bkhd->bqhd", probs.astype(BF), vh, preferred_element_type=F32)
    o = o.reshape(hidden.shape).astype(BF)
    y = dot(o, w["output_weight"], ((1,), (0,))) + w["output_bias"]
    ny, ry = norm_parts(y)
    mid = hidden + ny * w["sandwich_gain"] + w["sandwich_bias"]
    nm, rm = norm_parts(mid)
    c = (nm * w["second_gain"] + w["second_bias"]).astype(BF)
    f = dot(c, w["expand_weight"], ((1,), (0,))) + w["expand_bias"]
    g = jax.nn.gelu(f).astype(BF)
    e = dot(g, w["reduce_weight"], ((1,), (0,))) + w["reduce_bias"]
    ne, re = norm_parts(e)
    out = mid + ne * w["closing_gain"] + w["closing_bias"]
    kept = dict(n1=n1, r1=r1, a=a, qh=qh, kh=kh, vh=vh, probs=probs, o=o, y=y, ny=ny, ry=ry,
                nm=nm, rm=rm, c=c, f=f, g=g, e=e, ne=ne, re=re, out=out)
    return out, kept


def layer_back(dout, w, s, want_weights):
    sequences = s["qh"].shape[0]
    grads = {}
    de, grads["closing_gain"], grads["closing_bias"] = norm_back(dout, s["ne"], s["re"], w["closing_gain"])
    de = de.astype(BF)
    dg = dot(de, w["reduce_weight"], ((1,), (1,)))
    df = jax.vjp(jax.nn.gelu, s["f"])[1](dg)[0].astype(BF)
    dc = dot(df, w["expand_weight"], ((1,), (1,)))
    dmid, grads["second_gain"], grads["second_bias"] = norm_back(dc, s["nm"], s["rm"], w["second_gain"])
    dmid = dmid + dout
    dy, grads["sandwich_gain"], grads["sandwich_bias"] = norm_back(dmid, s["ny"], s["ry"], w["sandwich_gain"])
    dy = dy.astype(BF)
    do = heads_of(dot(dy, w["output_weight"], ((1,), (1,))).astype(BF), sequences)
    dprobs = jnp.einsum("bqhd,bkhd->bhqk", do, s["vh"], preferred_element_type=F32)
    dv = jnp.einsum("bhqk,bqhd->bkhd", s["probs"].astype(BF), do, preferred_element_type=F32)
    ds = RELAX * s["probs"] * (dprobs - jnp.sum(dprobs * s["probs"], axis=-1, keepdims=True))
    ds = ds.astype(BF)
    dq = jnp.einsum("bhqk,bkhd->bqhd", ds, s["kh"], preferred_element_type=F32)
    dk = jnp.einsum("bhqk,bqhd->bkhd", ds, s["qh"], preferred_element_type=F32)
    flat = dout.shape
    dmixed = jnp.concatenate([dq.reshape(flat) * QUERY_SCALE, dk.reshape(flat), dv.reshape(flat)], axis=1).astype(BF)
    da = dot(dmixed, w["joint_weight"], ((1,), (1,)))
    dh, grads["norm_gain"], grads["norm_bias"] = norm_back(da, s["n1"], s["r1"], w["norm_gain"])
    din = dmid + dh
    if not want_weights:
        return din, None
    model = flat[1]
    grads["reduce_weight"] = dot(s["g"], de, ((0,), (0,)))
    grads["reduce_bias"] = jnp.sum(de.astype(F32), axis=0)
    grads["expand_weight"] = dot(s["c"], df, ((0,), (0,)))
    grads["expand_bias"] = jnp.sum(df.astype(F32), axis=0)
    grads["output_weight"] = dot(s["o"], dy, ((0,), (0,)))
    grads["output_bias"] = jnp.sum(dy.astype(F32), axis=0)
    grads["joint_weight"] = dot(s["a"], dmixed, ((0,), (0,)))
    sums = jnp.sum(dmixed.astype(F32), axis=0)
    grads["joint_bias"] = jnp.concatenate([sums[:model], sums[2 * model :]])
    return din, grads


def passed_along(block, axis, distance):
    devices = range(lax.axis_size(axis))
    route = [(i - distance, i) for i in devices if i - distance in devices]
    return lax.ppermute(block, axis, route)


def local(tokens, lengths, *parameters):
    cotangent = parameters[-1]
    own = dict(zip(ORDER, parameters[:-1]))
    section = lax.axis_index("section")
    micro, rows, model = tokens.shape
    sequences = lengths.shape[1]
    slots = rows // sequences
    total = micro * rows

    packed = jnp.concatenate([own[name] for name in VECTORS], axis=1)
    packed = lax.all_gather(packed, "batch", axis=0, tiled=True).astype(F32)
    w = {}
    start = 0
    for name in VECTORS:
        width = own[name].shape[1]
        w[name] = packed[:, start : start + width].reshape(-1)
        start += width
    for name in MATRICES:
        w[name] = lax.all_gather(own[name], "batch", axis=1, tiled=True)[0]

    flat_lengths = lengths.reshape(-1)
    seen = lax.broadcasted_iota(jnp.int32, (micro * sequences, slots), 1) < flat_lengths[:, None]
    valid = seen.astype(F32).reshape(total, 1)
    source = tokens.reshape(total, model)
    first_out, _ = layer_fore(source, w, flat_lengths)
    incoming = passed_along(first_out.astype(BF), "section", 1)
    out, s = layer_fore(jnp.where(section == 0, source, incoming), w, flat_lengths)
    section_out = out.astype(BF).reshape(1, micro, rows, model)
    squares = jnp.stack([jnp.sum(s[name] * s[name] * valid) for name in ("y", "e", "out")])

    seed = cotangent.reshape(total, model).astype(F32) * valid
    last_in, _ = layer_back(seed, w, s, False)
    incoming = passed_along(last_in.astype(BF), "section", -1)
    din, grads = layer_back(jnp.where(section == 1, seed, incoming.astype(F32)), w, s, True)
    section_grad = din.reshape(1, micro, rows, model)

    result = {}
    for name in reversed(MATRICES):
        result[name] = lax.psum_scatter(grads[name].astype(BF)[None], "batch", scatter_dimension=1, tiled=True).astype(F32)
    devices = lax.axis_size("batch")
    small = jnp.concatenate([grads[name].reshape(devices, -1) for name in VECTORS], axis=1)
    small = lax.psum_scatter(small, "batch", scatter_dimension=0, tiled=True)
    start = 0
    for name in VECTORS:
        width = own[name].shape[1]
        result[name] = small[:, start : start + width]
        start += width
    count = jnp.sum(lengths).astype(F32)
    square_all, count_all = lax.psum((squares, count), "batch")
    magnitudes = jnp.sqrt(square_all / (count_all * model))[None]
    return (section_out, section_grad, magnitudes) + tuple(result[name] for name in ORDER)


def solution(mesh):
    vector, matrix = P("section", "batch"), P("section", "batch", None)
    kinds = tuple(matrix if name in MATRICES else vector for name in ORDER)
    rows = P(None, "batch", None)
    stacked = P("section", None, "batch", None)
    return jax.shard_map(
        local,
        mesh=mesh,
        in_specs=(rows, P(None, "batch")) + kinds + (rows,),
        out_specs=(stacked, stacked, P("section", None)) + kinds,
        check_vma=False,
    )
```

time: 2080 us -> 887 us (0.43)
  waiting for transfers between devices: 1460 us -> 618 us
  local copies, waits for them, and re-layouts: 167 us -> 37.9 us
  blocking collectives: 132 us -> 53.4 us
  other arithmetic: 100 us -> 37.4 us
  matrix products: 170 us -> 109 us
    unnamed x32 -> x10, waiting for transfers between devices: 640 us -> 21.9 us
    reduce_scatter x4, waiting for transfers between devices: 579 us -> 361 us  [local(): lax.psum_scatter(grads[name].astype(BF)[None], 'batch', scatter_dimension...]
    unnamed x120 -> x95, local copies, waits for them, and re-layouts: 80.5 us -> 4.81 us
    ppermute x4 -> x2, waiting for transfers between devices: 98.6 us -> 25.4 us  [passed_along(): return lax.ppermute(block, axis, route)]
    dot_general x38 -> x28, matrix products: 170 us -> 103 us  [the longest x18 89.2 us: dot(): lax.dot_general(left, right, (contract, ((), ())), preferred_element_type...]
    all_gather x4, waiting for transfers between devices: 146 us -> 210 us  [local(): w[name] = lax.all_gather(own[name], 'batch', axis=1, tiled=True)[0]]
    squeeze x1 -> x0, blocking collectives: 60.7 us -> none  [local(): weights = tuple((x[0] for x in gathered))]
    another operation x43 -> x0, local copies, waits for them, and re-layouts: 38.7 us -> none  [the longest x24 30.3 us: local(): kept_stack = jax.tree.map(lambda *x: jnp.stack(x), *kept_list)]
  transfers between devices with their start and end apart: 24 -> 11, of which waited for: 19 -> 11; matrix products, arithmetic and copies ran while one was open for 4% -> 8% of each run, Pallas kernels for 0% -> 0%
where the time goes in v1:
time: 887 us; the launch traced here: 877 us
  waiting for transfers between devices  618 us (70%)
  matrix products  109 us (12%)
  blocking collectives  53.4 us (6%)
  local copies, waits for them, and re-layouts  37.9 us (4%)
  other arithmetic  37.4 us (4%)
  between operations  16.4 us (2%)
    reduce_scatter x4, waiting for transfers between devices, local(): lax.psum_scatter(grads[name].astype(BF)[None], 'batch', scatter_dimension...  361 us
    all_gather x4, waiting for transfers between devices, local(): w[name] = lax.all_gather(own[name], 'batch', axis=1, tiled=True)[0]  210 us
    dot_general x18, matrix products, dot(): lax.dot_general(left, right, (contract, ((), ())), preferred_element_type...  89.2 us
    psum x1, blocking collectives, local(): square_all, count_all = lax.psum((squares, count), 'batch')  30 us
    ppermute x2, waiting for transfers between devices, passed_along(): return lax.ppermute(block, axis, route)  25.4 us
    all_gather x1, blocking collectives, local(): packed = lax.all_gather(packed, 'batch', axis=0, tiled=True).astype(F32)  23.4 us
    unnamed x10, waiting for transfers between devices  21.9 us
    reshape x13, local copies, waits for them, and re-layouts, heads_of(): return flat.reshape(sequences, flat.shape[0] // sequences, HEADS, HEAD_DIM)  19.3 us
  transfers between devices with their start and end apart: 11, of which 11 were waited for; matrix products, arithmetic and copies ran while one was open for 8% of the time, Pallas kernels for 0%

profile of v1, /device:TPU:0, one launch (start us, length us, event | category | flops | bytes accessed | tf_op | source)
XLA Modules:
  0.0 877.3 jit_solution(4646993037524076927)
XLA Ops:
  11.0 23.4 %all-gather = bf16[16,1,1024]{2,1,0:T(2,128)(2,1)S(1)} all-gather(bf16[1,1,1024]{2,1,0:T(2,128)(2,1)S(1)} %bitcast.277), channel_id=1, replica_groups=mesh['section'=2,'batch'=16] {'batch'}, dimensions={0}, use_global_device_ids=true | all-gather | bytes 34816 | tf_op jit(solution)/shard_map/all_gather | solution.py:145
  39.9 35.1 %all-gather.6.cloned.1.call-done = bf16[1,1024,3072]{2,1,0:T(8,128)(2,1)} async-done(((bf16[1,64,3072]{2,1,0:T(8,128)(2,1)}), bf16[1,1024,3072]{2,1,0:T(8,128)(2,1)}) %all-gather.6.cloned.1.call-update) | async-done | bytes 6291472 | tf_op jit(solution)/shard_map/all_gather | solution.py:153
  75.0 4.6 fusion.24
  83.9 4.0 fusion.210
  90.5 26.7 %all-gather.8.cloned.1.call-done = bf16[1,1024,1024]{2,1,0:T(8,128)(2,1)} async-done(((bf16[1,64,1024]{2,1,0:T(8,128)(2,1)}), bf16[1,1024,1024]{2,1,0:T(8,128)(2,1)}) %all-gather.8.cloned.1.call-update) | async-done | bytes 2097168 | tf_op jit(solution)/shard_map/all_gather | solution.py:153
  120.6 72.5 %all-gather.12.cloned.1.call-done = bf16[1,4096,1024]{2,1,0:T(8,128)(2,1)} async-done(((bf16[1,256,1024]{2,1,0:T(8,128)(2,1)}), bf16[1,4096,1024]{2,1,0:T(8,128)(2,1)}) %all-gather.12.cloned.1.call-update) | async-done | bytes 8388624 | tf_op jit(solution)/shard_map/all_gather | solution.py:153
  193.1 75.2 %all-gather.10.cloned.1.call-done = bf16[1,1024,4096]{2,1,0:T(8,128)(2,1)} async-done(((bf16[1,64,4096]{2,1,0:T(8,128)(2,1)}), bf16[1,1024,4096]{2,1,0:T(8,128)(2,1)}) %all-gather.10.cloned.1.call-update) | async-done | bytes 8388624 | tf_op jit(solution)/shard_map/all_gather | solution.py:153
  268.3 11.5 %fusion.216 = (f32[256]{0:T(256)S(1)}, f32[256,1024]{1,0:T(8,128)S(1)}) fusion(f32[1024]{0:T(1024)S(1)} %add.294, bf16[1,4096,1024]{2,1,0:T(8,128)(2,1)} %all-gather.12.cloned.1.call-done, bf16[1,1024,4096]{2,1,0:T(8,128)(2,1)} %all-gather.10.cloned.1.call-done, f32[4096]{0:T(1024)S(1)} %bitcast.278, f32[256,1024]{1,0:T(8,128)S(1)} %get-tuple-element.57, ...), kind=kOutput, calls=%fused_computation.295 | convolution fusion | flops 4307288064 | bytes 18906112 | tf_op jit(solution)/shard_map/dot_general | solution.py:31
  284.1 11.2 %collective-permute-done = bf16[256,1024]{1,0:T(8,128)(2,1)S(1)} collective-permute-done((bf16[256,1024]{1,0:T(8,128)(2,1)S(1)}, bf16[256,1024]{1,0:T(8,128)(2,1)S(1)}, u32[]{:S(2)}, u32[]{:S(2)}) %collective-permute-start) | collective-permute-done | bytes 524320 | tf_op jit(solution)/shard_map/ppermute | solution.py:132
  295.8 4.7 fusion.22
  315.1 6.2 fusion.29
  326.1 12.4 %fusion.204 = (f32[256]{0:T(256)S(1)}, f32[256]{0:T(256)S(1)}, f32[256,1024]{1,0:T(8,128)}) fusion(f32[256]{0:T(256)S(1)} %add_rsqrt_fusion.1, f32[256,1024]{1,0:T(8,128)S(1)} %get-tuple-element.53, f32[256]{0:T(256)S(1)} %broadcast_multiply_fusion.16, f32[1024]{0:T(1024)S(1)} %mul.546, bf16[1,1024,4096]{2,1,0:T(8,128)(2,1)} %all-gather.10.cloned.1.call-done, ...), kind=kOutput, calls=%fused_computation.288 | convolution fusion | flops 4317511680 | bytes 23601152 | tf_op jit(solution)/shard_map/dot_general | solution.py:31
  361.7 14.3 %collective-permute-done.1 = bf16[256,1024]{1,0:T(8,128)(2,1)} collective-permute-done((bf16[256,1024]{1,0:T(8,128)(2,1)}, bf16[256,1024]{1,0:T(8,128)(2,1)}, u32[]{:S(2)}, u32[]{:S(2)}) %collective-permute-start.1) | collective-permute-done | bytes 524320 | tf_op jit(solution)/shard_map/ppermute | solution.py:132
  376.0 3.6 multiply_reduce_fusion.2
  381.4 7.8 convert_reduce_fusion
  416.6 6.1 convert_bitcast_fusion.2
  423.0 7.3 convert_bitcast_fusion.1
  431.4 8.4 convert_bitcast_fusion
  443.8 30.0 %all-reduce.1 = (f32[3]{0:T(128)S(1)}, f32[]{:T(128)}) all-reduce(f32[3]{0:T(128)S(1)} %pad_maximum_fusion.1, f32[]{:T(128)S(6)} %convert_element_type.225), channel_id=1, replica_groups=mesh['section'=2,'batch'=16] {'batch'}, use_global_device_ids=true, to_apply=%region_41.42 | all-reduce | flops 4 | bytes 32 | tf_op jit(solution)/shard_map/psum | solution.py:183
  476.3 19.2 %all-reduce.4.cloned.1.call-done = f32[16,1024]{1,0:T(8,128)} async-done(((f32[16,1024]{1,0:T(8,128)}), f32[16,1024]{1,0:T(8,128)}) %all-reduce.4.cloned.1.call-update) | async-done | bytes 65552
  501.5 61.1 %reduce-scatter.7.cloned.1.call-done = bf16[1,64,1024]{2,1,0:T(8,128)(2,1)} async-done(((bf16[1,1024,1024]{2,1,0:T(8,128)(2,1)}), bf16[1,64,1024]{2,1,0:T(8,128)(2,1)}) %reduce-scatter.7.cloned.1.call-update) | async-done | bytes 131088 | tf_op jit(solution)/shard_map/reduce_scatter | solution.py:173
  564.3 86.6 %reduce-scatter.5.cloned.1.call-done = bf16[1,64,3072]{2,1,0:T(8,128)(2,1)} async-done(((bf16[1,1024,3072]{2,1,0:T(8,128)(2,1)}), bf16[1,64,3072]{2,1,0:T(8,128)(2,1)}) %reduce-scatter.5.cloned.1.call-update) | async-done | bytes 393232 | tf_op jit(solution)/shard_map/reduce_scatter | solution.py:173
  652.8 106.5 %reduce-scatter.9.cloned.1.call-done = bf16[1,64,4096]{2,1,0:T(8,128)(2,1)} async-done(((bf16[1,1024,4096]{2,1,0:T(8,128)(2,1)}), bf16[1,64,4096]{2,1,0:T(8,128)(2,1)}) %reduce-scatter.9.cloned.1.call-update) | async-done | bytes 524304 | tf_op jit(solution)/shard_map/reduce_scatter | solution.py:173
  761.4 107.0 %reduce-scatter.11.cloned.1.call-done = bf16[1,256,1024]{2,1,0:T(8,128)(2,1)} async-done(((bf16[1,4096,1024]{2,1,0:T(8,128)(2,1)}), bf16[1,256,1024]{2,1,0:T(8,128)(2,1)}) %reduce-scatter.11.cloned.1.call-update) | async-done | bytes 524304 | tf_op jit(solution)/shard_map/reduce_scatter | solution.py:173
  (261 shorter events, 115.4 us)
Async XLA Ops:
  7.2 67.8 %all-gather.6.cloned.1.call-start = ((), (), s32[]{:S(2)}) async-start(), calls=%async_computation.4 | async-start | bytes 6684672 | tf_op jit(solution)/shard_map/all_gather | solution.py:153
  7.9 109.3 %all-gather.8.cloned.1.call-start = ((), (), s32[]{:S(2)}) async-start(), calls=%async_computation.5 | async-start | bytes 2228224 | tf_op jit(solution)/shard_map/all_gather | solution.py:153
  8.7 184.4 %all-gather.12.cloned.1.call-start = ((), (), s32[]{:S(2)}) async-start(), calls=%async_computation.7 | async-start | bytes 8912896 | tf_op jit(solution)/shard_map/all_gather | solution.py:153
  9.4 258.9 %all-gather.10.cloned.1.call-start = ((), (), s32[]{:S(2)}) async-start(), calls=%async_computation.6 | async-start | bytes 8912896 | tf_op jit(solution)/shard_map/all_gather | solution.py:153
  10.0 485.5 %all-reduce.4.cloned.1.call-start = ((), (), s32[]{:S(2)}) async-start(), calls=%async_computation.12 | async-start | bytes 131072
  90.0 30.0 %copy-start.3 = (bf16[2,128,1024]{2,1,0:T(8,128)(2,1)S(1)}, bf16[2,128,1024]{2,1,0:T(8,128)(2,1)}, u32[]{:S(2)}) copy-start(bf16[2,128,1024]{2,1,0:T(8,128)(2,1)} %param.19) | copy-start | bytes 1572868
  268.3 15.5 %copy-start.31 = (s32[2,1]{0,1:T(1,128)S(1)}, s32[2,1]{0,1:T(1,128)}, u32[]{:S(2)}) copy-start(s32[2,1]{0,1:T(1,128)} %param.20) | copy-start | bytes 28
  268.3 15.6 %copy-start = (bf16[2,128,1024]{2,1,0:T(8,128)(2,1)S(1)}, bf16[2,128,1024]{2,1,0:T(8,128)(2,1)}, u32[]{:S(2)}) copy-start(bf16[2,128,1024]{2,1,0:T(8,128)(2,1)} %param.37) | copy-start | bytes 1572868
  280.3 15.0 %collective-permute-start = (bf16[256,1024]{1,0:T(8,128)(2,1)S(1)}, bf16[256,1024]{1,0:T(8,128)(2,1)S(1)}, u32[]{:S(2)}, u32[]{:S(2)}) collective-permute-start(bf16[256,1024]{1,0:T(8,128)(2,1)S(1)} %add_convert_fusion.3), channel_id=1, source_target_pairs={{0,16},{1,17},{2,18},{3,19},{4,20},{5,21},{6,22},{7,23},{8,24},{9,... | collective-permute-start | bytes 1572872 | tf_op jit(solution)/shard_map/ppermute | solution.py:132
  295.5 18.9 %copy-start.4 = (bf16[256,1024]{1,0:T(8,128)(2,1)}, bf16[256,1024]{1,0:T(8,128)(2,1)S(1)}, u32[]{:S(2)}) copy-start(bf16[256,1024]{1,0:T(8,128)(2,1)S(1)} %get-tuple-element.55) | copy-start | bytes 1572868
  306.6 6.1 copy-start.12
  308.1 4.6 copy-start.15
  314.4 6.9 slice-start
  315.1 6.2 slice-start.1
  360.4 15.6 %collective-permute-start.1 = (bf16[256,1024]{1,0:T(8,128)(2,1)}, bf16[256,1024]{1,0:T(8,128)(2,1)}, u32[]{:S(2)}, u32[]{:S(2)}) collective-permute-start(bf16[256,1024]{1,0:T(8,128)(2,1)} %fusion.121), channel_id=1, source_target_pairs={{16,0},{17,1},{18,2},{19,3},{20,4},{21,5},{22,6},{23,7},{24,8},{25... | collective-permute-start | bytes 1572872 | tf_op jit(solution)/shard_map/ppermute | solution.py:132
  361.7 19.7 %copy-start.34 = (f32[256,4096]{1,0:T(8,128)S(1)}, f32[256,4096]{1,0:T(8,128)}, u32[]{:S(2)}) copy-start(f32[256,4096]{1,0:T(8,128)} %copy-done.33) | copy-start | bytes 12582916
  376.0 13.2 %slice-start.2 = ((s8[8388608]{0:T(1024)(128)(4,1)}), s8[4194304]{0:T(1024)(128)(4,1)S(1)}, s32[]{:S(2)}) async-start(s8[8388608]{0:T(1024)(128)(4,1)} %bitcast.284), calls=%async_computation.15 | async-start | bytes 8388608
  381.3 7.8 copy-start.29
  381.4 7.8 slice-start.3
  413.5 149.2 %reduce-scatter.7.cloned.1.call-start = ((), (), s32[]{:S(2)}) async-start(), calls=%async_computation.9 | async-start | bytes 2228224 | tf_op jit(solution)/shard_map/reduce_scatter | solution.py:173
  416.6 234.3 %reduce-scatter.5.cloned.1.call-start = ((), (), s32[]{:S(2)}) async-start(), calls=%async_computation.8 | async-start | bytes 6684672 | tf_op jit(solution)/shard_map/reduce_scatter | solution.py:173
  422.8 336.5 %reduce-scatter.9.cloned.1.call-start = ((), (), s32[]{:S(2)}) async-start(), calls=%async_computation.10 | async-start | bytes 8912896 | tf_op jit(solution)/shard_map/reduce_scatter | solution.py:173
  430.4 438.1 %reduce-scatter.11.cloned.1.call-start = ((), (), s32[]{:S(2)}) async-start(), calls=%async_computation.11 | async-start | bytes 8912896 | tf_op jit(solution)/shard_map/reduce_scatter | solution.py:173
  439.8 35.1 %copy-start.25 = (f32[256,1024]{1,0:T(8,128)S(1)}, f32[256,1024]{1,0:T(8,128)}, u32[]{:S(2)}) copy-start(f32[256,1024]{1,0:T(8,128)} %get-tuple-element.108) | copy-start | bytes 3145732
  (30 other events, 77.3 us)
Sparse Core Ops, SparseCore 0:
  10.3 64.6 all-gather.5
  77.2 39.9 all-gather.7
  119.4 73.6 all-gather.11
  195.1 73.1 all-gather.9
  413.6 81.8 all-reduce.3
  499.5 63.1 reduce-scatter.6
  566.6 84.2 reduce-scatter.4
  655.5 103.8 reduce-scatter.8
  764.0 104.4 reduce-scatter.10

commit v2 on v1

v2 whole, which is shorter than its diff:
```python
import functools
import math
from typing import Any, NamedTuple

import jax
import jax.numpy as jnp
from jax import lax
from jax.experimental import pallas as pl
from jax.experimental.pallas import tpu as pltpu
from jax.sharding import PartitionSpec as P

HEADS = 16
HEAD_DIM = 64
EPSILON = 1e-05
RELAX = 32.0
MASKED = -1000000000.0
QUERY_SCALE = 1.0 / (RELAX * math.sqrt(HEAD_DIM))

BF = jnp.bfloat16
F32 = jnp.float32
VMEM_LIMIT = 62 * 2**20

MESH = pl.DeviceIdType.MESH
BLOCKS = 12
PART = 64
SLOTS = 4
GATHER_CROSSED = (3, 11)
SCATTER_ORDER = (8, 9, 10, 11, 4, 5, 6, 7, 3, 0, 1, 2)
UP, DOWN, SIDE = 0, 1, 2


def when(condition, action):
    if condition is True:
        action()
    else:
        pl.when(condition)(action)


def both(first, second):
    if first is True:
        return second
    if second is True:
        return first
    return first & second


class Place:
    def __init__(self, depth):
        index = lax.axis_index("batch")
        self.s = lax.axis_index("section")
        self.depth = depth
        self.z = index // 4
        self.x = (index // 2) % 2
        self.c = index % 2

    def device(self, z, x, c):
        return (self.s, (z * 2 + x) * 2 + c)

    def shard(self, z, x, c):
        return (z * 2 + x) * 2 + c

    def greet(self, across=False):
        z, x, c = self.z, self.x, self.c
        sem = pltpu.get_barrier_semaphore()

        def signal(device):
            pl.semaphore_signal(sem, inc=1, device_id=device, device_id_type=MESH)

        signal(self.device(z, 1 - x, c))
        signal(self.device(z, x, 1 - c))
        if across:
            signal((1 - self.s, self.shard(z, x, c)))
        pl.when(z < self.depth - 1)(lambda: signal(self.device(z + 1, x, c)))
        pl.when(z > 0)(lambda: signal(self.device(z - 1, x, c)))
        chain = (z < self.depth - 1).astype(jnp.int32) + (z > 0).astype(jnp.int32)
        pl.semaphore_wait(sem, (3 if across else 2) + chain)


def spot(item, shard):
    if item < 8:
        return item, pl.multiple_of(shard * PART, 16)
    return 8 + shard // 4, pl.multiple_of((shard % 4) * 4 * PART + (item - 8) * PART, 16)


def shard_view(refs, item, width):
    joint, output, expand, reduce = refs
    if item < 3:
        return joint.at[:, pl.ds(item * width, width)]
    if item == 3:
        return output
    if item < 8:
        return expand.at[:, pl.ds((item - 4) * width, width)]
    return reduce.at[pl.ds((item - 8) * PART, PART)]


class Gather:
    def __init__(self, place, own, store, sems):
        self.p, self.own, self.store = place, own, store
        self.send, self.share, self.recv, self.local = sems
        self.sent = []

    def at(self, item, shard):
        block, row = spot(item, shard)
        return self.store.at[block, pl.ds(row, PART)]

    def copy(self, item, shard, way, first=False):
        p = self.p
        target = self.at(item, shard)
        source = shard_view(self.own, item, self.store.shape[2]) if first else target
        recv = self.recv.at[item, shard]
        if way is None:
            send, device = self.share.at[item, shard // 2], p.device(p.z, p.x, 1 - p.c)
        else:
            send = self.send.at[item, shard // 2, way]
            device = (p.device(p.z + 1, p.x, p.c), p.device(p.z - 1, p.x, p.c), p.device(p.z, 1 - p.x, p.c))[way]
        return pltpu.make_async_remote_copy(source, target, send, recv, device_id=device, device_id_type=MESH)

    def go(self, item, shard, way, condition, first=False):
        self.sent.append((item, shard, way, condition, first))
        when(condition, lambda: self.copy(item, shard, way, first).start())

    def arrived(self, item, shard):
        self.copy(item, shard, None).wait_recv()

    def keep_own(self):
        me = self.p.shard(self.p.z, self.p.x, self.p.c)
        copies = [
            pltpu.make_async_copy(shard_view(self.own, item, self.store.shape[2]), self.at(item, me), self.local.at[item])
            for item in range(BLOCKS)
        ]
        for copy in copies:
            copy.start()
        return copies

    def own_sends(self, item):
        p = self.p
        me = p.shard(p.z, p.x, p.c)
        self.go(item, me, UP, p.z < p.depth - 1, True)
        self.go(item, me, DOWN, p.z > 0, True)
        self.go(item, me, SIDE, True, True)
        self.go(item, me, None, True, True)

    def chain_round(self, item, hop):
        p = self.p
        crossed = item in GATHER_CROSSED
        for x in (p.x, 1 - p.x) if crossed else (p.x,):
            for origin, present, way, onward in (
                (p.z - hop, p.z >= hop, UP, p.z < p.depth - 1),
                (p.z + hop, p.z + hop < p.depth, DOWN, p.z > 0),
            ):
                shard = p.shard(origin, x, p.c)
                when(present, lambda: self.arrived(item, shard))
                self.go(item, shard, way, both(present, onward))
                if not crossed:
                    self.go(item, shard, SIDE, present)
                self.go(item, shard, None, present)

    def side_own(self, item):
        p = self.p
        shard = p.shard(p.z, 1 - p.x, p.c)
        self.arrived(item, shard)
        if item in GATHER_CROSSED:
            self.go(item, shard, UP, p.z < p.depth - 1)
            self.go(item, shard, DOWN, p.z > 0)
        self.go(item, shard, None, True)

    def side_round(self, item, hop):
        p = self.p
        if item in GATHER_CROSSED:
            return
        for origin, present in ((p.z - hop, p.z >= hop), (p.z + hop, p.z + hop < p.depth)):
            shard = p.shard(origin, 1 - p.x, p.c)
            when(present, lambda: self.arrived(item, shard))
            self.go(item, shard, None, present)

    def rest(self, item):
        p = self.p
        for z in range(p.depth):
            for x in range(2):
                self.arrived(item, p.shard(z, x, 1 - p.c))

    def drain(self):
        for item, shard, way, condition, first in self.sent:
            when(condition, lambda: self.copy(item, shard, way, first).wait_send())


def run_gather(gather, ahead, ready):
    depth = gather.p.depth
    kept = gather.keep_own()
    for item in range(ahead):
        gather.own_sends(item)

    def finish(item):
        for hop in range(1, depth):
            gather.side_round(item, hop)
        gather.rest(item)
        kept[item].wait()
        ready(item)

    for item in range(BLOCKS):
        if item in GATHER_CROSSED:
            gather.side_own(item)
        for hop in range(1, depth):
            gather.chain_round(item, hop)
            if hop == 1:
                if item + ahead < BLOCKS:
                    gather.own_sends(item + ahead)
                if item not in GATHER_CROSSED:
                    gather.side_own(item)
        if item >= 1:
            finish(item - 1)
    finish(BLOCKS - 1)


def gather_sems(depth):
    kind = pltpu.SemaphoreType.DMA
    return [kind((BLOCKS, 2 * depth, 3)), kind((BLOCKS, 2 * depth)), kind((BLOCKS, 4 * depth)), kind((BLOCKS,))]


def total(*refs):
    value = refs[0][...].astype(F32)
    for ref in refs[1:]:
        value = value + ref[...].astype(F32)
    return value


class Scatter:
    def __init__(self, place, store, buffers, outs, sems):
        self.p, self.store, self.outs = place, store, outs
        self.core_in, self.side_in, self.chain_in = buffers
        (self.core_send, self.core_recv, self.side_send, self.side_recv, self.chain_send, self.chain_recv,
         self.core_free, self.side_free, self.chain_free) = sems
        depth = place.depth
        self.origins = [q for pair in zip(range(depth - 1, -1, -1), range(depth)) for q in pair][:depth]

    def mine(self, step, z, x, c):
        block, row = spot(SCATTER_ORDER[step], self.p.shard(z, x, c))
        return self.store.at[block, pl.ds(row, PART)]

    def core_copy(self, step, z, x):
        p, slot = self.p, step % SLOTS
        return pltpu.make_async_remote_copy(
            self.mine(step, z, x, 1 - p.c), self.core_in.at[slot, z * 2 + x],
            self.core_send.at[slot, z * 2 + x], self.core_recv.at[slot, z * 2 + x],
            device_id=p.device(p.z, p.x, 1 - p.c), device_id_type=MESH)

    def side_copy(self, step, z):
        p, slot = self.p, step % SLOTS
        return pltpu.make_async_remote_copy(
            self.mine(step, z, 1 - p.x, p.c), self.side_in.at[slot, z],
            self.side_send.at[slot, z], self.side_recv.at[slot, z],
            device_id=p.device(p.z, 1 - p.x, p.c), device_id_type=MESH)

    def chain_copy(self, step, z, up):
        p, slot = self.p, step % SLOTS
        return pltpu.make_async_remote_copy(
            self.mine(step, z, p.x, p.c), self.chain_in.at[slot, 1 - up, z],
            self.chain_send.at[slot, 1 - up, z], self.chain_recv.at[slot, 1 - up, z],
            device_id=p.device(p.z + 2 * up - 1, p.x, p.c), device_id_type=MESH)

    def core_stage(self, step):
        if step >= SLOTS:
            for z in self.origins:
                for x in range(2):
                    self.core_copy(step - SLOTS, z, x).wait_send()
            pl.semaphore_wait(self.core_free, 1)
        for z in self.origins:
            for x in range(2):
                self.core_copy(step, z, x).start()

    def from_core(self, step, z, x):
        self.core_copy(step, z, x).wait_recv()
        return self.core_in.at[step % SLOTS, z * 2 + x]

    def side_stage(self, step):
        p = self.p
        if step >= SLOTS:
            for z in self.origins:
                self.side_copy(step - SLOTS, z).wait_send()
            pl.semaphore_wait(self.side_free, 1)
        for z in self.origins:
            twin = self.from_core(step, z, 1 - p.x)
            mine = self.mine(step, z, 1 - p.x, p.c)
            mine[...] = total(mine, twin).astype(BF)
            self.side_copy(step, z).start()

    def chain_stage(self, step):
        p, slot, last = self.p, step % SLOTS, self.p.depth - 1
        if step >= SLOTS:
            for z in self.origins:
                up = (p.z < z).astype(jnp.int32)
                pl.when(p.z != z)(lambda: self.chain_copy(step - SLOTS, z, up).wait_send())
            pl.when(p.z < last)(lambda: pl.semaphore_wait(self.chain_free.at[0], 1))
            pl.when(p.z > 0)(lambda: pl.semaphore_wait(self.chain_free.at[1], 1))
        for z in self.origins:
            up = (p.z < z).astype(jnp.int32)
            fed = ((p.z < z) & (p.z > 0)) | ((p.z > z) & (p.z < last))

            @pl.when(p.z != z)
            def _():
                twin = self.from_core(step, z, p.x)
                mine = self.mine(step, z, p.x, p.c)
                self.side_copy(step, z).wait_recv()
                side = self.side_in.at[slot, z]

                @pl.when(fed)
                def _():
                    self.chain_copy(step, z, up).wait_recv()
                    mine[...] = total(mine, twin, side, self.chain_in.at[slot, 1 - up, z]).astype(BF)

                @pl.when(jnp.logical_not(fed))
                def _():
                    mine[...] = total(mine, twin, side).astype(BF)

                self.chain_copy(step, z, up).start()

    def own_stage(self, step):
        p, slot, last = self.p, step % SLOTS, self.p.depth - 1
        twin = self.from_core(step, p.z, p.x)
        self.side_copy(step, p.z).wait_recv()
        parts = [self.mine(step, p.z, p.x, p.c), twin, self.side_in.at[slot, p.z]]
        pl.when(p.z > 0)(lambda: self.chain_copy(step, p.z, 1).wait_recv())
        pl.when(p.z < last)(lambda: self.chain_copy(step, p.z, 0).wait_recv())
        below, above = self.chain_in.at[slot, 0, p.z], self.chain_in.at[slot, 1, p.z]
        out = self.outs[SCATTER_ORDER[step]]

        def put(*refs):
            out[...] = total(*refs)

        pl.when(p.z == 0)(lambda: put(*parts, above))
        pl.when(p.z == last)(lambda: put(*parts, below))
        pl.when((p.z > 0) & (p.z < last))(lambda: put(*parts, below, above))
        if step + SLOTS < BLOCKS:
            def signal(sem, device):
                pl.semaphore_signal(sem, inc=1, device_id=device, device_id_type=MESH)

            signal(self.core_free, p.device(p.z, p.x, 1 - p.c))
            signal(self.side_free, p.device(p.z, 1 - p.x, p.c))
            pl.when(p.z > 0)(lambda: signal(self.chain_free.at[0], p.device(p.z - 1, p.x, p.c)))
            pl.when(p.z < last)(lambda: signal(self.chain_free.at[1], p.device(p.z + 1, p.x, p.c)))

    def drain(self):
        p = self.p
        for step in range(BLOCKS - SLOTS, BLOCKS):
            for z in self.origins:
                for x in range(2):
                    self.core_copy(step, z, x).wait_send()
                self.side_copy(step, z).wait_send()
                up = (p.z < z).astype(jnp.int32)
                pl.when(p.z != z)(lambda: self.chain_copy(step, z, up).wait_send())


def run_scatter(scatter, ready):
    for tick in range(BLOCKS + 4):
        if tick < BLOCKS:
            ready(tick)
        if tick >= 4:
            scatter.own_stage(tick - 4)
        if tick < BLOCKS:
            scatter.core_stage(tick)
        if 1 <= tick <= BLOCKS:
            scatter.side_stage(tick - 1)
        if 2 <= tick < BLOCKS + 2:
            scatter.chain_stage(tick - 2)
    scatter.drain()


def scatter_scratch(depth, width):
    dma, plain = pltpu.SemaphoreType.DMA, pltpu.SemaphoreType.REGULAR
    return [
        pltpu.VMEM((SLOTS, 2 * depth, PART, width), BF),
        pltpu.VMEM((SLOTS, depth, PART, width), BF),
        pltpu.VMEM((SLOTS, 2, depth, PART, width), BF),
        dma((SLOTS, 2 * depth)), dma((SLOTS, 2 * depth)), dma((SLOTS, depth)), dma((SLOTS, depth)),
        dma((SLOTS, 2, depth)), dma((SLOTS, 2, depth)), plain, plain, plain((2,)),
    ]


class Layer(NamedTuple):
    norm_gain: Any
    norm_bias: Any
    joint_weight: Any
    joint_bias: Any
    output_weight: Any
    output_bias: Any
    sandwich_gain: Any
    sandwich_bias: Any
    second_gain: Any
    second_bias: Any
    expand_weight: Any
    expand_bias: Any
    reduce_weight: Any
    reduce_bias: Any
    closing_gain: Any
    closing_bias: Any


MATRICES = (2, 4, 10, 12)
VECTORS = tuple(i for i in range(16) if i not in MATRICES)


class Kept(NamedTuple):
    n1: Any
    r1: Any
    a: Any
    qh: Any
    kh: Any
    vh: Any
    probs: Any
    o: Any
    y: Any
    ny: Any
    ry: Any
    nm: Any
    rm: Any
    c: Any
    f: Any
    g: Any
    e: Any
    ne: Any
    re: Any
    out: Any


def dot(left, right, left_dim, right_dim):
    return lax.dot_general(left, right, (((left_dim,), (right_dim,)), ((), ())), preferred_element_type=F32)


def norm_parts(value):
    center = jnp.mean(value, axis=-1, keepdims=True)
    centered = value - center
    rate = lax.rsqrt(jnp.mean(centered * centered, axis=-1, keepdims=True) + EPSILON)
    return centered * rate, rate


def norm_back(grad, normal, rate, gain):
    scaled = grad * gain
    first = jnp.mean(scaled, axis=-1, keepdims=True)
    second = jnp.mean(scaled * normal, axis=-1, keepdims=True)
    gain_grad = jnp.sum(grad * normal, axis=0)
    bias_grad = jnp.sum(grad, axis=0)
    return rate * (scaled - first - normal * second), gain_grad, bias_grad


def heads_of(flat, sequences):
    return flat.reshape(sequences, flat.shape[0] // sequences, HEADS, HEAD_DIM)


def layer_fore(hidden_in, w, lengths):
    sequences = lengths.shape[0]
    model = hidden_in.shape[1]
    hidden = hidden_in.astype(F32)
    n1, r1 = norm_parts(hidden)
    a = (n1 * w.norm_gain + w.norm_bias).astype(BF)
    mixed = dot(a, w.joint_weight, 1, 0)
    q = ((mixed[:, :model] + w.joint_bias[:model]) * QUERY_SCALE).astype(BF)
    k = mixed[:, model : 2 * model].astype(BF)
    v = (mixed[:, 2 * model :] + w.joint_bias[model:]).astype(BF)
    qh, kh, vh = heads_of(q, sequences), heads_of(k, sequences), heads_of(v, sequences)
    scores = jnp.einsum("bqhd,bkhd->bhqk", qh, kh, preferred_element_type=F32)
    slots = scores.shape[-1]
    query_slot = lax.broadcasted_iota(jnp.int32, (sequences, slots, slots), 1)
    key_slot = lax.broadcasted_iota(jnp.int32, (sequences, slots, slots), 2)
    seen = (key_slot <= query_slot) & (key_slot < lengths[:, None, None])
    scores = jnp.where(seen[:, None], scores, MASKED)
    exponent = jnp.exp(RELAX * (scores - jnp.max(scores, axis=-1, keepdims=True)))
    probs = exponent / jnp.sum(exponent, axis=-1, keepdims=True)
    o = jnp.einsum("bhqk,bkhd->bqhd", probs.astype(BF), vh, preferred_element_type=F32)
    o = o.reshape(hidden.shape).astype(BF)
    y = dot(o, w.output_weight, 1, 0) + w.output_bias
    ny, ry = norm_parts(y)
    mid = hidden + ny * w.sandwich_gain + w.sandwich_bias
    nm, rm = norm_parts(mid)
    c = (nm * w.second_gain + w.second_bias).astype(BF)
    f = dot(c, w.expand_weight, 1, 0) + w.expand_bias
    g = jax.nn.gelu(f).astype(BF)
    e = dot(g, w.reduce_weight, 1, 0) + w.reduce_bias
    ne, re = norm_parts(e)
    out = mid + ne * w.closing_gain + w.closing_bias
    return out, Kept(n1, r1, a, qh, kh, vh, probs, o, y, ny, ry, nm, rm, c, f, g, e, ne, re, out)


def layer_back(dout, w, s, want_weights):
    sequences = s.qh.shape[0]
    de, closing_gain, closing_bias = norm_back(dout, s.ne, s.re, w.closing_gain)
    de = de.astype(BF)
    dg = dot(de, w.reduce_weight, 1, 1)
    df = jax.vjp(jax.nn.gelu, s.f)[1](dg)[0].astype(BF)
    dc = dot(df, w.expand_weight, 1, 1)
    dmid, second_gain, second_bias = norm_back(dc, s.nm, s.rm, w.second_gain)
    dmid = dmid + dout
    dy, sandwich_gain, sandwich_bias = norm_back(dmid, s.ny, s.ry, w.sandwich_gain)
    dy = dy.astype(BF)
    do = heads_of(dot(dy, w.output_weight, 1, 1).astype(BF), sequences)
    dprobs = jnp.einsum("bqhd,bkhd->bhqk", do, s.vh, preferred_element_type=F32)
    dv = jnp.einsum("bhqk,bqhd->bkhd", s.probs.astype(BF), do, preferred_element_type=F32)
    ds = RELAX * s.probs * (dprobs - jnp.sum(dprobs * s.probs, axis=-1, keepdims=True))
    ds = ds.astype(BF)
    dq = jnp.einsum("bhqk,bkhd->bqhd", ds, s.kh, preferred_element_type=F32)
    dk = jnp.einsum("bhqk,bqhd->bkhd", ds, s.qh, preferred_element_type=F32)
    flat = dout.shape
    dmixed = jnp.concatenate([dq.reshape(flat) * QUERY_SCALE, dk.reshape(flat), dv.reshape(flat)], axis=1).astype(BF)
    da = dot(dmixed, w.joint_weight, 1, 1)
    dh, norm_gain, norm_bias = norm_back(da, s.n1, s.r1, w.norm_gain)
    din = dmid + dh
    if not want_weights:
        return din, None
    model = flat[1]
    sums = jnp.sum(dmixed.astype(F32), axis=0)
    return din, Layer(
        norm_gain=norm_gain,
        norm_bias=norm_bias,
        joint_weight=dot(s.a, dmixed, 0, 0),
        joint_bias=jnp.concatenate([sums[:model], sums[2 * model :]]),
        output_weight=dot(s.o, dy, 0, 0),
        output_bias=jnp.sum(dy.astype(F32), axis=0),
        sandwich_gain=sandwich_gain,
        sandwich_bias=sandwich_bias,
        second_gain=second_gain,
        second_bias=second_bias,
        expand_weight=dot(s.c, df, 0, 0),
        expand_bias=jnp.sum(df.astype(F32), axis=0),
        reduce_weight=dot(s.g, de, 0, 0),
        reduce_bias=jnp.sum(de.astype(F32), axis=0),
        closing_gain=closing_gain,
        closing_bias=closing_bias,
    )


def passed_along(block, axis, distance):
    devices = range(lax.axis_size(axis))
    route = [(i - distance, i) for i in devices if i - distance in devices]
    return lax.ppermute(block, axis, route)


def local(gather_matrices, scatter_matrices, tokens, lengths, *parameters):
    cotangent = parameters[-1]
    own = parameters[:-1]
    section = lax.axis_index("section")
    micro, rows, model = tokens.shape
    sequences = lengths.shape[1]
    slots = rows // sequences
    total_rows = micro * rows

    packed = jnp.concatenate([own[i] for i in VECTORS], axis=1)
    packed = lax.all_gather(packed, "batch", axis=0, tiled=True).astype(F32)
    w = list(own)
    start = 0
    for i in VECTORS:
        width = own[i].shape[1]
        w[i] = packed[:, start : start + width].reshape(-1)
        start += width
    for i, whole in zip(MATRICES, gather_matrices([own[i] for i in MATRICES])):
        w[i] = whole
    w = Layer(*w)

    flat_lengths = lengths.reshape(-1)
    seen = lax.broadcasted_iota(jnp.int32, (micro * sequences, slots), 1) < flat_lengths[:, None]
    valid = seen.astype(F32).reshape(total_rows, 1)
    source = tokens.reshape(total_rows, model)
    first_out, _ = layer_fore(source, w, flat_lengths)
    incoming = passed_along(first_out.astype(BF), "section", 1)
    out, s = layer_fore(jnp.where(section == 0, source, incoming), w, flat_lengths)
    section_out = out.astype(BF).reshape(1, micro, rows, model)
    squares = jnp.stack([jnp.sum(part * part * valid) for part in (s.y, s.e, s.out)])

    seed = cotangent.reshape(total_rows, model).astype(F32) * valid
    last_in, _ = layer_back(seed, w, s, False)
    incoming = passed_along(last_in.astype(BF), "section", -1)
    din, grads = layer_back(jnp.where(section == 1, seed, incoming.astype(F32)), w, s, True)
    section_grad = din.reshape(1, micro, rows, model)

    result = list(grads)
    for i, part in zip(MATRICES, scatter_matrices([grads[i].astype(BF) for i in MATRICES])):
        result[i] = part
    devices = lax.axis_size("batch")
    small = jnp.concatenate([grads[i].reshape(devices, -1) for i in VECTORS], axis=1)
    small = lax.psum_scatter(small, "batch", scatter_dimension=0, tiled=True)
    start = 0
    for i in VECTORS:
        width = own[i].shape[1]
        result[i] = small[:, start : start + width]
        start += width
    count = jnp.sum(lengths).astype(F32)
    square_all, count_all = lax.psum((squares, count), "batch")
    magnitudes = jnp.sqrt(square_all / (count_all * model))[None]
    return (section_out, section_grad, magnitudes) + tuple(result)


def plain_gather(shards):
    return [lax.all_gather(w, "batch", axis=1, tiled=True)[0] for w in shards]


def plain_scatter(grads):
    return [lax.psum_scatter(g[None], "batch", scatter_dimension=1, tiled=True).astype(F32) for g in grads]


def gather_kernel(depth, *refs):
    own, store, sems = refs[:4], refs[4], refs[5:]
    place = Place(depth)
    place.greet()
    gather = Gather(place, own, store, sems)
    run_gather(gather, 2, lambda item: None)
    gather.drain()


def ring_gather(depth, shards):
    width = shards[1].shape[2]
    whole = pl.pallas_call(
        functools.partial(gather_kernel, depth),
        out_shape=jax.ShapeDtypeStruct((BLOCKS, width, width), BF),
        in_specs=[pl.BlockSpec(memory_space=pl.ANY)] * 4,
        out_specs=pl.BlockSpec(memory_space=pl.ANY),
        scratch_shapes=gather_sems(depth),
        compiler_params=pltpu.CompilerParams(collective_id=1, has_side_effects=True, vmem_limit_bytes=VMEM_LIMIT),
        name="gather",
    )(*[w[0] for w in shards])
    return (
        jnp.concatenate([whole[i] for i in range(3)], axis=1),
        whole[3],
        jnp.concatenate([whole[i] for i in range(4, 8)], axis=1),
        whole[8:].reshape(4 * width, width),
    )


def scatter_kernel(depth, store, joint, output, expand, reduce, *scratch):
    place = Place(depth)
    place.greet()
    outs = [shard_view((joint, output, expand, reduce), item, store.shape[2]) for item in range(BLOCKS)]
    run_scatter(Scatter(place, store, scratch[:3], outs, scratch[3:]), lambda step: None)


def ring_scatter(depth, grads):
    joint, output, expand, reduce = grads
    width = output.shape[1]
    store = jnp.concatenate([
        joint.reshape(width, 3, width).swapaxes(0, 1), output[None],
        expand.reshape(width, 4, width).swapaxes(0, 1), reduce.reshape(4, width, width)])
    shapes = ((PART, 3 * width), (PART, width), (PART, 4 * width), (4 * PART, width))
    parts = pl.pallas_call(
        functools.partial(scatter_kernel, depth),
        out_shape=[jax.ShapeDtypeStruct(shape, F32) for shape in shapes],
        in_specs=[pl.BlockSpec(memory_space=pltpu.VMEM)],
        out_specs=[pl.BlockSpec(memory_space=pltpu.VMEM)] * 4,
        scratch_shapes=scatter_scratch(depth, width),
        compiler_params=pltpu.CompilerParams(collective_id=2, has_side_effects=True, vmem_limit_bytes=VMEM_LIMIT),
        name="scatter",
    )(store)
    return [part[None] for part in parts]


def solution(mesh):
    vector, matrix = P("section", "batch"), P("section", "batch", None)
    kinds = tuple(matrix if i in MATRICES else vector for i in range(16))
    rows = P(None, "batch", None)
    stacked = P("section", None, "batch", None)
    devices = mesh.shape["batch"]
    if devices == 16:
        ways = functools.partial(ring_gather, devices // 4), functools.partial(ring_scatter, devices // 4)
    else:
        ways = plain_gather, plain_scatter
    return jax.shard_map(
        functools.partial(local, *ways),
        mesh=mesh,
        in_specs=(rows, P(None, "batch")) + kinds + (rows,),
        out_specs=(stacked, stacked, P("section", None)) + kinds,
        check_vma=False,
    )
```

time: 887 us -> 686 us (0.77)
  waiting for transfers between devices: 618 us -> 24.9 us
  Pallas kernels: 0 us -> 315 us
  local copies, waits for them, and re-layouts: 37.9 us -> 104 us
    reduce_scatter x4 -> x0, waiting for transfers between devices: 361 us -> none  [local(): lax.psum_scatter(grads[name].astype(BF)[None], 'batch', scatter_dimension...]
    pallas_call x0 -> x2, Pallas kernels: none -> 315 us  [the longest x1 166 us: ring_scatter(): pl.pallas_call(functools.partial(scatter_kernel, depth), out_shape=[jax.S...]
    all_gather x4 -> x0, waiting for transfers between devices: 210 us -> none  [local(): w[name] = lax.all_gather(own[name], 'batch', axis=1, tiled=True)[0]]
    unnamed x10 -> x2, waiting for transfers between devices: 21.9 us -> 0.04 us
    concatenate x1 -> x2, other arithmetic: 0.01 us -> 20.9 us  [the longest x1 20.9 us: ring_scatter(): jnp.concatenate([joint.reshape(width, 3, width).swapaxes(0, 1), output[No...]
    convert_element_type x0 -> x2, local copies, waits for them, and re-layouts: none -> 20.5 us  [local(): grads[i].astype(BF)]
    reshape x11 -> x13, local copies, waits for them, and re-layouts: 0.7 us -> 20.8 us  [the longest x1 11.5 us: ring_scatter(): expand.reshape(width, 4, width).swapaxes(0, 1)]
    squeeze x0 -> x1, local copies, waits for them, and re-layouts: none -> 11 us  [ring_gather(): whole[i]]
  transfers between devices with their start and end apart: 11 -> 3, of which waited for: 11 -> 2; matrix products, arithmetic and copies ran while one was open for 8% -> 6% of each run, Pallas kernels for 0% -> 24%
where the time goes in v2:
time: 686 us; the launch traced here: 679 us
  Pallas kernels  315 us (46%)
  matrix products  112 us (16%)
  local copies, waits for them, and re-layouts  104 us (15%)
  blocking collectives  56 us (8%)
  other arithmetic  46 us (7%)
  waiting for transfers between devices  24.9 us (4%)
  between operations  16.7 us (2%)
    pallas_call x1, Pallas kernels, ring_scatter(): pl.pallas_call(functools.partial(scatter_kernel, depth), out_shape=[jax.S...  166 us
    pallas_call x1, Pallas kernels, ring_gather(): pl.pallas_call(functools.partial(gather_kernel, depth), out_shape=jax.Sha...  149 us
    dot_general x18, matrix products, dot(): lax.dot_general(left, right, (((left_dim,), (right_dim,)), ((), ())), pre...  93.2 us
    psum x1, blocking collectives, local(): square_all, count_all = lax.psum((squares, count), 'batch')  32.8 us
    ppermute x2, waiting for transfers between devices, passed_along(): return lax.ppermute(block, axis, route)  24.9 us
    all_gather x1, blocking collectives, local(): packed = lax.all_gather(packed, 'batch', axis=0, tiled=True).astype(F32)  23.2 us
    concatenate x1, other arithmetic, ring_scatter(): jnp.concatenate([joint.reshape(width, 3, width).swapaxes(0, 1), output[No...  20.9 us
    convert_element_type x2, local copies, waits for them, and re-layouts, local(): grads[i].astype(BF)  20.5 us
  transfers between devices with their start and end apart: 3, of which 2 were waited for; matrix products, arithmetic and copies ran while one was open for 6% of the time, Pallas kernels for 24%

profile of v2, /device:TPU:0, one launch (start us, length us, event | category | flops | bytes accessed | tf_op | source)
XLA Modules:
  0.0 679.1 jit_solution(754946267973115152)
XLA Ops:
  8.2 23.2 %all-gather = bf16[16,1,1024]{2,1,0:T(2,128)(2,1)S(1)} all-gather(bf16[1,1,1024]{2,1,0:T(2,128)(2,1)S(1)} %bitcast.255), channel_id=1, replica_groups=mesh['section'=2,'batch'=16] {'batch'}, dimensions={0}, use_global_device_ids=true | all-gather | bytes 34816 | tf_op jit(solution)/shard_map/all_gather | solution.py:546
  31.5 148.9 %gather.1 = bf16[12,1024,1024]{2,1,0:T(8,128)(2,1)} custom-call(bf16[64,3072]{1,0:T(8,128)(2,1)} %bitcast.252, bf16[64,1024]{1,0:T(8,128)(2,1)} %bitcast.254, bf16[64,4096]{1,0:T(8,128)(2,1)} %bitcast.242, bf16[256,1024]{1,0:T(8,128)(2,1)} %bitcast.243), custom_call_target="tpu_custom_call" | custom-call | tf_op jit(solution)/shard_map/gather/pallas_call | solution.py:609
  180.4 11.0 %slice_bitcast_fusion.3 = (bf16[1024,1024]{1,0:T(8,128)(2,1)}, bf16[1024,1024]{1,0:T(8,128)(2,1)}, bf16[1024,1024]{1,0:T(8,128)(2,1)}, bf16[1024,1024]{1,0:T(8,1...) fusion(bf16[12,1024,1024]{2,1,0:T(8,128)(2,1)} %gather.1), kind=kLoop, calls=%fused_computation.49 | loop fusion | bytes 29360128 | tf_op jit(solution)/shard_map/squeeze | solution.py:621
  191.4 7.6 %slice.176 = bf16[4,1024,1024]{2,1,0:T(8,128)(2,1)} slice(bf16[12,1024,1024]{2,1,0:T(8,128)(2,1)} %gather.1), slice={[8:12], [0:1024], [0:1024]} | slice | bytes 16777216 | tf_op jit(solution)/shard_map/slice | solution.py:622
  199.7 4.8 fusion.104
  208.9 3.7 fusion.176
  219.0 13.3 %fusion.182 = (f32[256]{0:T(256)S(1)}, f32[256,1024]{1,0:T(8,128)S(1)}) fusion(f32[1024]{0:T(1024)S(1)} %add.284, bf16[4096,1024]{1,0:T(8,128)(2,1)} %bitcast.222, f32[4096]{0:T(1024)S(1)} %bitcast.256, f32[256,1024]{1,0:T(8,128)S(1)} %get-tuple-element.67, f32[1024]{0:T(1024)S(1)} %add.276, f32[1024]{0:T(1024)S(1)} %mul.542, f32[256]{0:T(256)S(1)} %add_rsqrt_fusion.5, ...), kind=kOutput, calls=%fused_computation.298 | convolution fusion | flops 4340842496 | bytes 18906112 | tf_op jit(solution)/shard_map/dot_general | solution.py:426
  237.7 12.1 %collective-permute-done = bf16[256,1024]{1,0:T(8,128)(2,1)S(1)} collective-permute-done((bf16[256,1024]{1,0:T(8,128)(2,1)}, bf16[256,1024]{1,0:T(8,128)(2,1)S(1)}, u32[]{:S(2)}, u32[]{:S(2)}) %collective-permute-start) | collective-permute-done | bytes 524320 | tf_op jit(solution)/shard_map/ppermute | solution.py:533
  250.3 4.8 fusion.163
  270.2 4.7 convolution_add_fusion
  274.9 5.1 fusion.185
  281.9 15.6 %fusion.169 = (f32[256]{0:T(256)S(1)}, f32[256]{0:T(256)S(1)}, f32[256,1024]{1,0:T(8,128)}) fusion(f32[256]{0:T(256)S(1)} %add_rsqrt_fusion.1, f32[256,1024]{1,0:T(8,128)S(1)} %get-tuple-element.63, f32[256]{0:T(256)S(1)} %broadcast_multiply_fusion.16, f32[1024]{0:T(1024)S(1)} %mul.542, bf16[1024,1024]{1,0:T(8,128)(2,1)} %get-tuple-element.69, ...), kind=kOutput, calls=%fused_computation.291 | convolution fusion | flops 4351066112 | bytes 23601152 | tf_op jit(solution)/shard_map/dot_general | solution.py:426
  324.8 12.8 %collective-permute-done.1 = bf16[256,1024]{1,0:T(8,128)(2,1)} collective-permute-done((bf16[256,1024]{1,0:T(8,128)(2,1)}, bf16[256,1024]{1,0:T(8,128)(2,1)}, u32[]{:S(2)}, u32[]{:S(2)}) %collective-permute-start.1) | collective-permute-done | bytes 524320 | tf_op jit(solution)/shard_map/ppermute | solution.py:533
  342.9 7.7 %convert_reduce_fusion = (f32[4096]{0:T(1024)S(1)}, bf16[256,4096]{1,0:T(8,128)(2,1)S(1)}) fusion(f32[256,4096]{1,0:T(8,128)S(1)} %copy-done.47, bf16[256,1024]{1,0:T(8,128)(2,1)S(1)} %get-tuple-element.55, bf16[4096,1024]{1,0:T(8,128)(2,1)} %bitcast.224), kind=kOutput, calls=%fused_computation.25 | convolution fusion | flops 2170548224 | bytes 15220736 | tf_op jit(solution)/shard_map/dot_general | solution.py:426
  371.6 5.7 convolution_convert_fusion.1
  377.3 5.4 convolution_convert_fusion
  384.7 4.8 convolution_convert_fusion.2
  393.1 8.6 %copy.146 = bf16[1024,3072]{0,1:T(8,128)(2,1)} copy(bf16[1024,3072]{1,0:T(8,128)(2,1)} %convolution_convert_fusion.2) | data formatting | bytes 12582912 | tf_op jit(solution)/shard_map/convert_element_type | solution.py:574
  401.7 8.6 %copy.147 = bf16[1024,3,1024]{2,0,1:T(8,128)(2,1)} copy(bf16[1024,3,1024]{0,2,1:T(8,128)(2,1)} %bitcast.221) | data formatting | bytes 12582912 | tf_op jit(solution)/shard_map/reshape | solution.py:637
  410.3 11.9 %copy.148 = bf16[1024,4096]{0,1:T(8,128)(2,1)} copy(bf16[1024,4096]{1,0:T(8,128)(2,1)} %convolution_convert_fusion.1) | data formatting | bytes 16777216 | tf_op jit(solution)/shard_map/convert_element_type | solution.py:574
  425.7 11.5 %copy.149 = bf16[1024,4,1024]{2,0,1:T(8,128)(2,1)} copy(bf16[1024,4,1024]{0,2,1:T(8,128)(2,1)} %bitcast.218) | data formatting | bytes 16777216 | tf_op jit(solution)/shard_map/reshape | solution.py:638
  437.2 32.8 %all-reduce.1 = (f32[3]{0:T(128)S(1)}, f32[]{:T(128)}) all-reduce(f32[3]{0:T(128)S(1)} %pad_maximum_fusion.4, f32[]{:T(128)S(6)} %convert_element_type.208), channel_id=1, replica_groups=mesh['section'=2,'batch'=16] {'batch'}, use_global_device_ids=true, to_apply=%region_41.42 | all-reduce | flops 4 | bytes 32 | tf_op jit(solution)/shard_map/psum | solution.py:585
  472.0 20.9 %pad_maximum_fusion.store = bf16[12,1024,1024]{2,1,0:T(8,128)(2,1)} fusion(bf16[4,1024,1024]{2,1,0:T(8,128)(2,1)} %bitcast.229, bf16[4,1024,1024]{2,1,0:T(8,128)(2,1)} %bitcast.219, bf16[1,1024,1024]{2,1,0:T(8,128)(2,1)} %convert_bitcast_fusion, bf16[3,1024,1024]{2,1,0:T(8,128)(2,1)} %bitcast.220), kind=kLoop, calls=%fused_computation.2 | loop fusion | flops 37748736 | bytes 50331648 | tf_op jit(solution)/shard_map/concatenate | solution.py:636
  493.5 165.7 %scatter.1 = (f32[64,3072]{1,0:T(8,128)}, f32[64,1024]{1,0:T(8,128)}, f32[64,4096]{1,0:T(8,128)}, f32[256,1024]{1,0:T(8,128)}) custom-call(bf16[12,1024,1024]{2,1,0:T(8,128)(2,1)} %pad_maximum_fusion.store), custom_call_target="tpu_custom_call" | custom-call | tf_op jit(solution)/shard_map/scatter/pallas_call | solution.py:640
  (258 shorter events, 111.0 us)
Async XLA Ops:
  7.2 652.0 %all-reduce.4.cloned.1.call-start = ((), (), s32[]{:S(2)}) async-start(), calls=%async_computation | async-start | bytes 131072
  191.4 7.8 %copy-start.9 = (bf16[2,128,1024]{2,1,0:T(8,128)(2,1)S(1)}, bf16[2,128,1024]{2,1,0:T(8,128)(2,1)}, u32[]{:S(2)}) copy-start(bf16[2,128,1024]{2,1,0:T(8,128)(2,1)} %param.19) | copy-start | bytes 1572868
  219.0 18.3 %copy-start = (bf16[2,128,1024]{2,1,0:T(8,128)(2,1)S(1)}, bf16[2,128,1024]{2,1,0:T(8,128)(2,1)}, u32[]{:S(2)}) copy-start(bf16[2,128,1024]{2,1,0:T(8,128)(2,1)} %param.37) | copy-start | bytes 1572868
  233.8 15.9 %collective-permute-start = (bf16[256,1024]{1,0:T(8,128)(2,1)}, bf16[256,1024]{1,0:T(8,128)(2,1)S(1)}, u32[]{:S(2)}, u32[]{:S(2)}) collective-permute-start(bf16[256,1024]{1,0:T(8,128)(2,1)} %add_convert_fusion.6), channel_id=1, source_target_pairs={{0,16},{1,17},{2,18},{3,19},{4,20},{5,21},{6,22},{7,23},{8,24},{9,... | collective-permute-start | bytes 1572872 | tf_op jit(solution)/shard_map/ppermute | solution.py:533
  250.0 18.9 %copy-start.3 = (bf16[256,1024]{1,0:T(8,128)(2,1)}, bf16[256,1024]{1,0:T(8,128)(2,1)S(1)}, u32[]{:S(2)}) copy-start(bf16[256,1024]{1,0:T(8,128)(2,1)S(1)} %get-tuple-element.65) | copy-start | bytes 1572868
  256.9 6.5 copy-start.10
  268.8 6.0 slice-start
  270.2 4.7 slice-start.1
  274.9 5.4 copy-start.1
  318.4 5.9 copy-start.46
  321.7 16.0 %collective-permute-start.1 = (bf16[256,1024]{1,0:T(8,128)(2,1)}, bf16[256,1024]{1,0:T(8,128)(2,1)}, u32[]{:S(2)}, u32[]{:S(2)}) collective-permute-start(bf16[256,1024]{1,0:T(8,128)(2,1)} %fusion.75), channel_id=1, source_target_pairs={{16,0},{17,1},{18,2},{19,3},{20,4},{21,5},{22,6},{23,7},{24,8},{25... | collective-permute-start | bytes 1572872 | tf_op jit(solution)/shard_map/ppermute | solution.py:533
  324.3 18.6 %copy-start.47 = (f32[256,4096]{1,0:T(8,128)S(1)}, f32[256,4096]{1,0:T(8,128)}, u32[]{:S(2)}) copy-start(f32[256,4096]{1,0:T(8,128)} %convolution_add_fusion) | copy-start | bytes 12582916
  342.9 7.8 %copy-start.43 = (bf16[256,1024]{1,0:T(8,128)(2,1)}, bf16[256,1024]{1,0:T(8,128)(2,1)S(1)}, u32[]{:S(2)}) copy-start(bf16[256,1024]{1,0:T(8,128)(2,1)S(1)} %get-tuple-element.55) | copy-start | bytes 1572868
  342.9 7.8 %copy-start.24 = (bf16[1024,1024]{1,0:T(8,128)(2,1)S(1)}, bf16[1024,1024]{1,0:T(8,128)(2,1)}, u32[]{:S(2)}) copy-start(bf16[1024,1024]{1,0:T(8,128)(2,1)} %get-tuple-element.68) | copy-start | bytes 6291460
  342.9 7.8 %copy-start.26 = (bf16[1024,1024]{1,0:T(8,128)(2,1)S(1)}, bf16[1024,1024]{1,0:T(8,128)(2,1)}, u32[]{:S(2)}) copy-start(bf16[1024,1024]{1,0:T(8,128)(2,1)} %get-tuple-element.69) | copy-start | bytes 6291460
  342.9 7.8 %copy-start.28 = (bf16[1024,1024]{1,0:T(8,128)(2,1)S(1)}, bf16[1024,1024]{1,0:T(8,128)(2,1)}, u32[]{:S(2)}) copy-start(bf16[1024,1024]{1,0:T(8,128)(2,1)} %get-tuple-element.70) | copy-start | bytes 6291460
  342.9 7.8 %copy-start.30 = (bf16[1024,1024]{1,0:T(8,128)(2,1)S(1)}, bf16[1024,1024]{1,0:T(8,128)(2,1)}, u32[]{:S(2)}) copy-start(bf16[1024,1024]{1,0:T(8,128)(2,1)} %get-tuple-element.71) | copy-start | bytes 6291460
  371.6 5.7 copy-start.44
  371.6 5.7 copy-start.48
  384.6 5.3 copy-start.18
  384.6 5.3 copy-start.20
  384.7 5.3 copy-start.22
  425.7 44.9 %copy-start.37 = (f32[256,1024]{1,0:T(8,128)S(1)}, f32[256,1024]{1,0:T(8,128)}, u32[]{:S(2)}) copy-start(f32[256,1024]{1,0:T(8,128)} %get-tuple-element.127) | copy-start | bytes 3145732
  659.2 11.9 %copy-start.39 = (f32[256,1024]{1,0:T(8,128)S(1)}, f32[256,1024]{1,0:T(8,128)}, u32[]{:S(2)}) copy-start(f32[256,1024]{1,0:T(8,128)} %get-tuple-element.26) | copy-start | bytes 3145732
  (30 other events, 74.7 us)
Sparse Core Ops, SparseCore 0:
  423.8 84.3 all-reduce.3

commit v3 on v1

v3 whole, which is shorter than its diff:
```python
import functools
import math
from typing import Any, NamedTuple

import jax
import jax.numpy as jnp
from jax import lax
from jax.experimental import pallas as pl
from jax.experimental.pallas import tpu as pltpu
from jax.sharding import PartitionSpec as P

HEADS = 16
HEAD_DIM = 64
EPSILON = 1e-05
RELAX = 32.0
MASKED = -1000000000.0
QUERY_SCALE = 1.0 / (RELAX * math.sqrt(HEAD_DIM))

BF = jnp.bfloat16
F32 = jnp.float32
VMEM_LIMIT = 62 * 2**20

class Params(NamedTuple):
    norm_gain: Any
    norm_bias: Any
    joint_weight: Any
    joint_bias: Any
    output_weight: Any
    output_bias: Any
    sandwich_gain: Any
    sandwich_bias: Any
    second_gain: Any
    second_bias: Any
    expand_weight: Any
    expand_bias: Any
    reduce_weight: Any
    reduce_bias: Any
    closing_gain: Any
    closing_bias: Any


MATRICES = (2, 4, 10, 12)
VECTORS = tuple(i for i in range(16) if i not in MATRICES)


class Kept(NamedTuple):
    n1: Any
    r1: Any
    a: Any
    qh: Any
    kh: Any
    vh: Any
    probs: Any
    o: Any
    y: Any
    ny: Any
    ry: Any
    nm: Any
    rm: Any
    c: Any
    f: Any
    g: Any
    e: Any
    ne: Any
    re: Any
    out: Any


def dot(left, right, left_dim, right_dim):
    return lax.dot_general(left, right, (((left_dim,), (right_dim,)), ((), ())), preferred_element_type=F32)


def norm_parts(value):
    center = jnp.mean(value, axis=-1, keepdims=True)
    centered = value - center
    rate = lax.rsqrt(jnp.mean(centered * centered, axis=-1, keepdims=True) + EPSILON)
    return centered * rate, rate


def norm_back(grad, normal, rate, gain):
    scaled = grad * gain
    first = jnp.mean(scaled, axis=-1, keepdims=True)
    second = jnp.mean(scaled * normal, axis=-1, keepdims=True)
    gain_grad = jnp.sum(grad * normal, axis=0)
    bias_grad = jnp.sum(grad, axis=0)
    return rate * (scaled - first - normal * second), gain_grad, bias_grad


def heads_of(flat, sequences):
    return flat.reshape(sequences, flat.shape[0] // sequences, HEADS, HEAD_DIM)


def layer_fore(hidden_in, w, lengths):
    sequences = lengths.shape[0]
    model = hidden_in.shape[1]
    hidden = hidden_in.astype(F32)
    n1, r1 = norm_parts(hidden)
    a = (n1 * w.norm_gain + w.norm_bias).astype(BF)
    mixed = dot(a, w.joint_weight, 1, 0)
    q = ((mixed[:, :model] + w.joint_bias[:model]) * QUERY_SCALE).astype(BF)
    k = mixed[:, model : 2 * model].astype(BF)
    v = (mixed[:, 2 * model :] + w.joint_bias[model:]).astype(BF)
    qh, kh, vh = heads_of(q, sequences), heads_of(k, sequences), heads_of(v, sequences)
    scores = jnp.einsum("bqhd,bkhd->bhqk", qh, kh, preferred_element_type=F32)
    slots = scores.shape[-1]
    query_slot = lax.broadcasted_iota(jnp.int32, (sequences, slots, slots), 1)
    key_slot = lax.broadcasted_iota(jnp.int32, (sequences, slots, slots), 2)
    seen = (key_slot <= query_slot) & (key_slot < lengths[:, None, None])
    scores = jnp.where(seen[:, None], scores, MASKED)
    exponent = jnp.exp(RELAX * (scores - jnp.max(scores, axis=-1, keepdims=True)))
    probs = exponent / jnp.sum(exponent, axis=-1, keepdims=True)
    o = jnp.einsum("bhqk,bkhd->bqhd", probs.astype(BF), vh, preferred_element_type=F32)
    o = o.reshape(hidden.shape).astype(BF)
    y = dot(o, w.output_weight, 1, 0) + w.output_bias
    ny, ry = norm_parts(y)
    mid = hidden + ny * w.sandwich_gain + w.sandwich_bias
    nm, rm = norm_parts(mid)
    c = (nm * w.second_gain + w.second_bias).astype(BF)
    f = dot(c, w.expand_weight, 1, 0) + w.expand_bias
    g = jax.nn.gelu(f).astype(BF)
    e = dot(g, w.reduce_weight, 1, 0) + w.reduce_bias
    ne, re = norm_parts(e)
    out = mid + ne * w.closing_gain + w.closing_bias
    return out, Kept(n1, r1, a, qh, kh, vh, probs, o, y, ny, ry, nm, rm, c, f, g, e, ne, re, out)


def layer_back(dout, w, s, want_weights):
    sequences = s.qh.shape[0]
    de, closing_gain, closing_bias = norm_back(dout, s.ne, s.re, w.closing_gain)
    de = de.astype(BF)
    dg = dot(de, w.reduce_weight, 1, 1)
    df = jax.vjp(jax.nn.gelu, s.f)[1](dg)[0].astype(BF)
    dc = dot(df, w.expand_weight, 1, 1)
    dmid, second_gain, second_bias = norm_back(dc, s.nm, s.rm, w.second_gain)
    dmid = dmid + dout
    dy, sandwich_gain, sandwich_bias = norm_back(dmid, s.ny, s.ry, w.sandwich_gain)
    dy = dy.astype(BF)
    do = heads_of(dot(dy, w.output_weight, 1, 1).astype(BF), sequences)
    dprobs = jnp.einsum("bqhd,bkhd->bhqk", do, s.vh, preferred_element_type=F32)
    dv = jnp.einsum("bhqk,bqhd->bkhd", s.probs.astype(BF), do, preferred_element_type=F32)
    ds = RELAX * s.probs * (dprobs - jnp.sum(dprobs * s.probs, axis=-1, keepdims=True))
    ds = ds.astype(BF)
    dq = jnp.einsum("bhqk,bkhd->bqhd", ds, s.kh, preferred_element_type=F32)
    dk = jnp.einsum("bhqk,bqhd->bkhd", ds, s.qh, preferred_element_type=F32)
    flat = dout.shape
    dmixed = jnp.concatenate([dq.reshape(flat) * QUERY_SCALE, dk.reshape(flat), dv.reshape(flat)], axis=1).astype(BF)
    da = dot(dmixed, w.joint_weight, 1, 1)
    dh, norm_gain, norm_bias = norm_back(da, s.n1, s.r1, w.norm_gain)
    din = dmid + dh
    if not want_weights:
        return din, None
    model = flat[1]
    sums = jnp.sum(dmixed.astype(F32), axis=0)
    return din, Params(
        norm_gain=norm_gain,
        norm_bias=norm_bias,
        joint_weight=dot(s.a, dmixed, 0, 0),
        joint_bias=jnp.concatenate([sums[:model], sums[2 * model :]]),
        output_weight=dot(s.o, dy, 0, 0),
        output_bias=jnp.sum(dy.astype(F32), axis=0),
        sandwich_gain=sandwich_gain,
        sandwich_bias=sandwich_bias,
        second_gain=second_gain,
        second_bias=second_bias,
        expand_weight=dot(s.c, df, 0, 0),
        expand_bias=jnp.sum(df.astype(F32), axis=0),
        reduce_weight=dot(s.g, de, 0, 0),
        reduce_bias=jnp.sum(de.astype(F32), axis=0),
        closing_gain=closing_gain,
        closing_bias=closing_bias,
    )


def passed_along(block, axis, distance):
    devices = range(lax.axis_size(axis))
    route = [(i - distance, i) for i in devices if i - distance in devices]
    return lax.ppermute(block, axis, route)


def plain_local(tokens, lengths, *parameters):
    cotangent = parameters[-1]
    own = parameters[:-1]
    section = lax.axis_index("section")
    micro, rows, model = tokens.shape
    sequences = lengths.shape[1]
    slots = rows // sequences
    total_rows = micro * rows

    packed = jnp.concatenate([own[i] for i in VECTORS], axis=1)
    packed = lax.all_gather(packed, "batch", axis=0, tiled=True).astype(F32)
    w = list(own)
    start = 0
    for i in VECTORS:
        width = own[i].shape[1]
        w[i] = packed[:, start : start + width].reshape(-1)
        start += width
    for i, whole in zip(MATRICES, plain_gather([own[i] for i in MATRICES])):
        w[i] = whole
    w = Params(*w)

    flat_lengths = lengths.reshape(-1)
    seen = lax.broadcasted_iota(jnp.int32, (micro * sequences, slots), 1) < flat_lengths[:, None]
    valid = seen.astype(F32).reshape(total_rows, 1)
    source = tokens.reshape(total_rows, model)
    first_out, _ = layer_fore(source, w, flat_lengths)
    incoming = passed_along(first_out.astype(BF), "section", 1)
    out, s = layer_fore(jnp.where(section == 0, source, incoming), w, flat_lengths)
    section_out = out.astype(BF).reshape(1, micro, rows, model)
    squares = jnp.stack([jnp.sum(part * part * valid) for part in (s.y, s.e, s.out)])

    seed = cotangent.reshape(total_rows, model).astype(F32) * valid
    last_in, _ = layer_back(seed, w, s, False)
    incoming = passed_along(last_in.astype(BF), "section", -1)
    din, grads = layer_back(jnp.where(section == 1, seed, incoming.astype(F32)), w, s, True)
    section_grad = din.reshape(1, micro, rows, model)

    result = list(grads)
    for i, part in zip(MATRICES, plain_scatter([grads[i].astype(BF) for i in MATRICES])):
        result[i] = part
    devices = lax.axis_size("batch")
    small = jnp.concatenate([grads[i].reshape(devices, -1) for i in VECTORS], axis=1)
    small = lax.psum_scatter(small, "batch", scatter_dimension=0, tiled=True)
    start = 0
    for i in VECTORS:
        width = own[i].shape[1]
        result[i] = small[:, start : start + width]
        start += width
    count = jnp.sum(lengths).astype(F32)
    square_all, count_all = lax.psum((squares, count), "batch")
    magnitudes = jnp.sqrt(square_all / (count_all * model))[None]
    return (section_out, section_grad, magnitudes) + tuple(result)


def plain_gather(shards):
    return [lax.all_gather(w, "batch", axis=1, tiled=True)[0] for w in shards]


def plain_scatter(grads):
    return [lax.psum_scatter(g[None], "batch", scatter_dimension=1, tiled=True).astype(F32) for g in grads]


MESH = pl.DeviceIdType.MESH
BLOCKS = 12
VECTOR_ITEM = 12
PART = 64
SLOTS = 4
GATHER_ORDER = (VECTOR_ITEM,) + tuple(range(BLOCKS))
GATHER_CROSSED = (3, 11)
GATHER_AHEAD = 3
SCATTER_ORDER = (8, 9, 10, 11, 4, 5, 6, 7, 3, 0, 1, 2)
UP, DOWN, SIDE = 0, 1, 2


def when(condition, action):
    if condition is True:
        action()
    else:
        pl.when(condition)(action)


def both(first, second):
    if first is True:
        return second
    if second is True:
        return first
    return first & second


class Place:
    def __init__(self, depth):
        index = lax.axis_index("batch")
        self.s = lax.axis_index("section")
        self.depth = depth
        self.z = index // 4
        self.x = (index // 2) % 2
        self.c = index % 2

    def device(self, z, x, c):
        return (self.s, (z * 2 + x) * 2 + c)

    def shard(self, z, x, c):
        return (z * 2 + x) * 2 + c

    def me(self):
        return self.shard(self.z, self.x, self.c)

    def across(self):
        return (1 - self.s, self.me())

    def greet(self):
        z, x, c = self.z, self.x, self.c
        sem = pltpu.get_barrier_semaphore()

        def signal(device):
            pl.semaphore_signal(sem, inc=1, device_id=device, device_id_type=MESH)

        signal(self.device(z, 1 - x, c))
        signal(self.device(z, x, 1 - c))
        signal(self.across())
        pl.when(z < self.depth - 1)(lambda: signal(self.device(z + 1, x, c)))
        pl.when(z > 0)(lambda: signal(self.device(z - 1, x, c)))
        chain = (z < self.depth - 1).astype(jnp.int32) + (z > 0).astype(jnp.int32)
        pl.semaphore_wait(sem, 3 + chain)


def spot(item, shard):
    if item < 8:
        return item, pl.multiple_of(shard * PART, 16)
    return 8 + shard // 4, pl.multiple_of((shard % 4) * 4 * PART + (item - 8) * PART, 16)


def shard_view(refs, item, width):
    joint, output, expand, reduce, vectors = refs
    if item < 3:
        return joint.at[:, pl.ds(item * width, width)]
    if item == 3:
        return output
    if item < 8:
        return expand.at[:, pl.ds((item - 4) * width, width)]
    if item < VECTOR_ITEM:
        return reduce.at[pl.ds((item - 8) * PART, PART)]
    return vectors


class Gather:
    def __init__(self, place, own, store, vectors, sems):
        self.p, self.own, self.store, self.vectors = place, own, store, vectors
        self.send, self.share, self.recv, self.local = sems
        self.sent = []

    def at(self, item, shard):
        if item == VECTOR_ITEM:
            return self.vectors.at[shard]
        block, row = spot(item, shard)
        return self.store.at[block, pl.ds(row, PART)]

    def copy(self, item, shard, way, first=False):
        p = self.p
        target = self.at(item, shard)
        source = shard_view(self.own, item, self.store.shape[2]) if first else target
        recv = self.recv.at[item, shard]
        if way is None:
            send, device = self.share.at[item, shard // 2], p.device(p.z, p.x, 1 - p.c)
        else:
            send = self.send.at[item, shard // 2, way]
            device = (p.device(p.z + 1, p.x, p.c), p.device(p.z - 1, p.x, p.c), p.device(p.z, 1 - p.x, p.c))[way]
        return pltpu.make_async_remote_copy(source, target, send, recv, device_id=device, device_id_type=MESH)

    def go(self, item, shard, way, condition, first=False):
        self.sent.append((item, shard, way, condition, first))
        when(condition, lambda: self.copy(item, shard, way, first).start())

    def arrived(self, item, shard):
        self.copy(item, shard, None).wait_recv()

    def keep_own(self):
        me = self.p.me()
        copies = [
            pltpu.make_async_copy(shard_view(self.own, item, self.store.shape[2]), self.at(item, me), self.local.at[item])
            for item in range(BLOCKS + 1)
        ]
        for copy in copies:
            copy.start()
        return copies

    def own_sends(self, item):
        p = self.p
        self.go(item, p.me(), UP, p.z < p.depth - 1, True)
        self.go(item, p.me(), DOWN, p.z > 0, True)
        self.go(item, p.me(), SIDE, True, True)
        self.go(item, p.me(), None, True, True)

    def chain_round(self, item, hop):
        p = self.p
        crossed = item in GATHER_CROSSED
        for x in (p.x, 1 - p.x) if crossed else (p.x,):
            for origin, present, way, onward in (
                (p.z - hop, p.z >= hop, UP, p.z < p.depth - 1),
                (p.z + hop, p.z + hop < p.depth, DOWN, p.z > 0),
            ):
                shard = p.shard(origin, x, p.c)
                when(present, lambda: self.arrived(item, shard))
                self.go(item, shard, way, both(present, onward))
                if not crossed:
                    self.go(item, shard, SIDE, present)
                self.go(item, shard, None, present)

    def side_own(self, item):
        p = self.p
        shard = p.shard(p.z, 1 - p.x, p.c)
        self.arrived(item, shard)
        if item in GATHER_CROSSED:
            self.go(item, shard, UP, p.z < p.depth - 1)
            self.go(item, shard, DOWN, p.z > 0)
        self.go(item, shard, None, True)

    def side_round(self, item, hop):
        p = self.p
        if item in GATHER_CROSSED:
            return
        for origin, present in ((p.z - hop, p.z >= hop), (p.z + hop, p.z + hop < p.depth)):
            shard = p.shard(origin, 1 - p.x, p.c)
            when(present, lambda: self.arrived(item, shard))
            self.go(item, shard, None, present)

    def rest(self, item):
        p = self.p
        for z in range(p.depth):
            for x in range(2):
                self.arrived(item, p.shard(z, x, 1 - p.c))

    def drain(self):
        for item, shard, way, condition, first in self.sent:
            when(condition, lambda: self.copy(item, shard, way, first).wait_send())


def run_gather(gather, ready):
    depth, count = gather.p.depth, len(GATHER_ORDER)
    kept = gather.keep_own()
    for item in GATHER_ORDER[:GATHER_AHEAD]:
        gather.own_sends(item)

    def finish(item):
        for hop in range(1, depth):
            gather.side_round(item, hop)
        gather.rest(item)
        kept[item].wait()
        ready(item)

    for place, item in enumerate(GATHER_ORDER):
        if item in GATHER_CROSSED:
            gather.side_own(item)
        for hop in range(1, depth):
            gather.chain_round(item, hop)
            if hop == 1:
                if place + GATHER_AHEAD < count:
                    gather.own_sends(GATHER_ORDER[place + GATHER_AHEAD])
                if item not in GATHER_CROSSED:
                    gather.side_own(item)
        if place >= 1:
            finish(GATHER_ORDER[place - 1])
    finish(GATHER_ORDER[-1])


def gather_sems(depth):
    kind, items = pltpu.SemaphoreType.DMA, BLOCKS + 1
    return [kind((items, 2 * depth, 3)), kind((items, 2 * depth)), kind((items, 4 * depth)), kind((items,))]


def total(*refs):
    value = refs[0][...].astype(F32)
    for ref in refs[1:]:
        value = value + ref[...].astype(F32)
    return value


class Scatter:
    def __init__(self, place, part, count, slots, buffers, outs, sems):
        self.p, self.part, self.count, self.slots, self.outs = place, part, count, slots, outs
        self.core_in, self.side_in, self.chain_in = buffers
        (self.core_send, self.core_recv, self.side_send, self.side_recv, self.chain_send, self.chain_recv,
         self.core_free, self.side_free, self.chain_free) = sems
        depth = place.depth
        self.origins = [q for pair in zip(range(depth - 1, -1, -1), range(depth)) for q in pair][:depth]

    def mine(self, step, z, x, c):
        return self.part(step, self.p.shard(z, x, c))

    def core_copy(self, step, z, x):
        p, slot = self.p, step % self.slots
        return pltpu.make_async_remote_copy(
            self.mine(step, z, x, 1 - p.c), self.core_in.at[slot, z * 2 + x],
            self.core_send.at[slot, z * 2 + x], self.core_recv.at[slot, z * 2 + x],
            device_id=p.device(p.z, p.x, 1 - p.c), device_id_type=MESH)

    def side_copy(self, step, z):
        p, slot = self.p, step % self.slots
        return pltpu.make_async_remote_copy(
            self.mine(step, z, 1 - p.x, p.c), self.side_in.at[slot, z],
            self.side_send.at[slot, z], self.side_recv.at[slot, z],
            device_id=p.device(p.z, 1 - p.x, p.c), device_id_type=MESH)

    def chain_copy(self, step, z, up):
        p, slot = self.p, step % self.slots
        return pltpu.make_async_remote_copy(
            self.mine(step, z, p.x, p.c), self.chain_in.at[slot, 1 - up, z],
            self.chain_send.at[slot, 1 - up, z], self.chain_recv.at[slot, 1 - up, z],
            device_id=p.device(p.z + 2 * up - 1, p.x, p.c), device_id_type=MESH)

    def core_stage(self, step):
        if step >= self.slots:
            for z in self.origins:
                for x in range(2):
                    self.core_copy(step - self.slots, z, x).wait_send()
            pl.semaphore_wait(self.core_free, 1)
        for z in self.origins:
            for x in range(2):
                self.core_copy(step, z, x).start()

    def from_core(self, step, z, x):
        self.core_copy(step, z, x).wait_recv()
        return self.core_in.at[step % self.slots, z * 2 + x]

    def side_stage(self, step):
        p = self.p
        if step >= self.slots:
            for z in self.origins:
                self.side_copy(step - self.slots, z).wait_send()
            pl.semaphore_wait(self.side_free, 1)
        for z in self.origins:
            twin = self.from_core(step, z, 1 - p.x)
            mine = self.mine(step, z, 1 - p.x, p.c)
            mine[...] = total(mine, twin).astype(mine.dtype)
            self.side_copy(step, z).start()

    def chain_stage(self, step):
        p, slot, last = self.p, step % self.slots, self.p.depth - 1
        if step >= self.slots:
            for z in self.origins:
                up = (p.z < z).astype(jnp.int32)
                pl.when(p.z != z)(lambda: self.chain_copy(step - self.slots, z, up).wait_send())
            pl.when(p.z < last)(lambda: pl.semaphore_wait(self.chain_free.at[0], 1))
            pl.when(p.z > 0)(lambda: pl.semaphore_wait(self.chain_free.at[1], 1))
        for z in self.origins:
            up = (p.z < z).astype(jnp.int32)
            fed = ((p.z < z) & (p.z > 0)) | ((p.z > z) & (p.z < last))

            @pl.when(p.z != z)
            def _():
                twin = self.from_core(step, z, p.x)
                mine = self.mine(step, z, p.x, p.c)
                self.side_copy(step, z).wait_recv()
                side = self.side_in.at[slot, z]

                @pl.when(fed)
                def _():
                    self.chain_copy(step, z, up).wait_recv()
                    mine[...] = total(mine, twin, side, self.chain_in.at[slot, 1 - up, z]).astype(mine.dtype)

                @pl.when(jnp.logical_not(fed))
                def _():
                    mine[...] = total(mine, twin, side).astype(mine.dtype)

                self.chain_copy(step, z, up).start()

    def own_stage(self, step):
        p, slot, last = self.p, step % self.slots, self.p.depth - 1
        twin = self.from_core(step, p.z, p.x)
        self.side_copy(step, p.z).wait_recv()
        parts = [self.mine(step, p.z, p.x, p.c), twin, self.side_in.at[slot, p.z]]
        pl.when(p.z > 0)(lambda: self.chain_copy(step, p.z, 1).wait_recv())
        pl.when(p.z < last)(lambda: self.chain_copy(step, p.z, 0).wait_recv())
        below, above = self.chain_in.at[slot, 0, p.z], self.chain_in.at[slot, 1, p.z]
        out = self.outs[step]

        def put(*refs):
            out[...] = total(*refs)

        pl.when(p.z == 0)(lambda: put(*parts, above))
        pl.when(p.z == last)(lambda: put(*parts, below))
        pl.when((p.z > 0) & (p.z < last))(lambda: put(*parts, below, above))
        if step + self.slots < self.count:
            def signal(sem, device):
                pl.semaphore_signal(sem, inc=1, device_id=device, device_id_type=MESH)

            signal(self.core_free, p.device(p.z, p.x, 1 - p.c))
            signal(self.side_free, p.device(p.z, 1 - p.x, p.c))
            pl.when(p.z > 0)(lambda: signal(self.chain_free.at[0], p.device(p.z - 1, p.x, p.c)))
            pl.when(p.z < last)(lambda: signal(self.chain_free.at[1], p.device(p.z + 1, p.x, p.c)))

    def drain(self):
        p = self.p
        for step in range(self.count - self.slots, self.count):
            for z in self.origins:
                for x in range(2):
                    self.core_copy(step, z, x).wait_send()
                self.side_copy(step, z).wait_send()
                up = (p.z < z).astype(jnp.int32)
                pl.when(p.z != z)(lambda: self.chain_copy(step, z, up).wait_send())


def run_scatter(scatter, vector_scatter, ready):
    for tick in range(BLOCKS + 4):
        if tick < BLOCKS:
            ready(tick)
        if tick >= 4:
            scatter.own_stage(tick - 4)
        if tick < BLOCKS:
            scatter.core_stage(tick)
        if 1 <= tick <= BLOCKS:
            scatter.side_stage(tick - 1)
        if 2 <= tick < BLOCKS + 2:
            scatter.chain_stage(tick - 2)
        if tick == BLOCKS - 1:
            vector_scatter.core_stage(0)
        if tick == BLOCKS:
            vector_scatter.side_stage(0)
        if tick == BLOCKS + 1:
            vector_scatter.chain_stage(0)
    vector_scatter.own_stage(0)
    scatter.drain()
    vector_scatter.drain()


def scatter_scratch(depth, slots, rows, width, dtype):
    dma, plain = pltpu.SemaphoreType.DMA, pltpu.SemaphoreType.REGULAR
    return [
        pltpu.VMEM((slots, 2 * depth, rows, width), dtype),
        pltpu.VMEM((slots, depth, rows, width), dtype),
        pltpu.VMEM((slots, 2, depth, rows, width), dtype),
        dma((slots, 2 * depth)), dma((slots, 2 * depth)), dma((slots, depth)), dma((slots, depth)),
        dma((slots, 2, depth)), dma((slots, 2, depth)), plain, plain, plain((2,)),
    ]


(NORM_GAIN, NORM_BIAS, OUTPUT_BIAS, SANDWICH_GAIN, SANDWICH_BIAS, SECOND_GAIN, SECOND_BIAS, REDUCE_BIAS,
 CLOSING_GAIN, CLOSING_BIAS, QUERY_BIAS, VALUE_BIAS, EXPAND_BIAS) = range(13)
NARROW = 10
VECTOR_ROWS = 16
FIGURES = 13
LANES = 128
TILE = 256
CHUNK = 32
CURVE = math.sqrt(2.0 / math.pi)
BEND = 0.044715


class Work(NamedTuple):
    vec: Any
    dvec: Any
    h: Any
    a: Any
    q: Any
    k: Any
    v: Any
    p: Any
    o: Any
    n_h: Any
    r_h: Any
    n_y: Any
    r_y: Any
    n_m: Any
    r_m: Any
    n_e: Any
    r_e: Any
    mid: Any
    c: Any
    g: Any
    slope: Any
    de: Any
    dy: Any
    do: Any
    din: Any
    sums: Any


def mxu(left, right, left_dim, right_dim):
    return lax.dot_general(left, right, (((left_dim,), (right_dim,)), ((), ())), preferred_element_type=F32)


def mean_of(value):
    return jnp.mean(value, axis=-1, keepdims=True)


def norm_of(value):
    centered = value - mean_of(value)
    rate = lax.rsqrt(mean_of(centered * centered) + EPSILON)
    return centered * rate, rate


def norm_pull(grad, normal, rate, gain):
    scaled = grad * gain
    return rate * (scaled - mean_of(scaled) - normal * mean_of(scaled * normal))


def column_sum(value):
    return jnp.sum(value, axis=0, keepdims=True)


class Layer:
    def __init__(self, work, store, lengths):
        self.w, self.store, self.lengths = work, store, lengths
        self.tokens, self.width = work.h.shape
        self.sequences = lengths.shape[0]
        self.slots = self.tokens // self.sequences

    def row(self, index):
        return self.w.vec[index : index + 1, :]

    def add(self, index, value):
        self.w.dvec[index : index + 1, :] += value

    def chunks(self, body, first=0, last=None):
        last = self.tokens if last is None else last

        def step(i, carry):
            body(pl.ds(pl.multiple_of(i * CHUNK, CHUNK), CHUNK), i)
            return carry

        lax.fori_loop(first // CHUNK, last // CHUNK, step, 0)

    def tiles(self, body):
        def step(i, carry):
            body(pl.ds(pl.multiple_of(i * TILE, TILE), TILE))
            return carry

        lax.fori_loop(0, self.width // TILE, step, 0)

    def valid(self, i):
        per = self.slots // CHUNK
        slot = (i % per) * CHUNK + lax.broadcasted_iota(jnp.int32, (CHUNK, 1), 0)
        return jnp.where(slot < self.lengths[i // per], 1.0, 0.0)


    def fore_start(self, source, first=0, last=None):
        w = self.w

        def body(rows, i):
            h = source[rows, :]
            w.h[rows, :] = h
            normal, rate = norm_of(h.astype(F32))
            w.n_h[rows, :] = normal
            w.r_h[rows, :] = rate
            w.a[rows, :] = (normal * self.row(NORM_GAIN) + self.row(NORM_BIAS)).astype(BF)

        self.chunks(body, first, last)

    def fore_joint(self, block):
        w = self.w
        bias = (QUERY_BIAS, None, VALUE_BIAS)[block]
        target = (w.q, w.k, w.v)[block]

        def body(tile):
            mixed = mxu(w.a[...], self.store[block, :, tile], 1, 0)
            if bias is not None:
                mixed = mixed + w.vec[bias : bias + 1, tile]
            if block == 0:
                mixed = mixed * QUERY_SCALE
            target[:, tile] = mixed.astype(BF)

        self.tiles(body)

    def pairs(self, body):
        count = self.width // LANES

        def step(i, carry):
            sequence, pair = i // count, i % count
            rows = pl.ds(pl.multiple_of(sequence * self.slots, self.slots), self.slots)
            lanes = pl.ds(pl.multiple_of(pair * LANES, LANES), LANES)
            body(rows, lanes, i, self.lengths[sequence])
            return carry

        lax.fori_loop(0, self.sequences * count, step, 0, unroll=2)

    def split(self, value):
        low = lax.broadcasted_iota(jnp.int32, value.shape, 1) < HEAD_DIM
        zero = jnp.zeros_like(value)
        return jnp.concatenate([jnp.where(low, value, zero), jnp.where(low, zero, value)], axis=0)

    def fore_attention(self):
        w, slots = self.w, self.slots

        def body(rows, lanes, i, length):
            scores = mxu(self.split(w.q[rows, lanes]), w.k[rows, lanes], 1, 1)
            query = lax.broadcasted_iota(jnp.int32, (2 * slots, slots), 0) % slots
            key = lax.broadcasted_iota(jnp.int32, (2 * slots, slots), 1)
            scores = jnp.where((key <= query) & (key < length), scores, MASKED)
            weight = jnp.exp(RELAX * (scores - jnp.max(scores, axis=-1, keepdims=True)))
            probs = (weight / jnp.sum(weight, axis=-1, keepdims=True)).astype(BF)
            w.p[i] = probs
            wide = jnp.concatenate([probs[:slots], probs[slots:]], axis=1)
            w.o[rows, lanes] = mxu(wide, self.split(w.v[rows, lanes]), 1, 0).astype(BF)

        self.pairs(body)

    def fore_output(self):
        w = self.w

        def body(tile):
            w.n_y[:, tile] = mxu(w.o[...], self.store[3, :, tile], 1, 0) + w.vec[OUTPUT_BIAS : OUTPUT_BIAS + 1, tile]

        self.tiles(body)

        def middle(rows, i):
            y = w.n_y[rows, :]
            w.sums[0:1, :] += column_sum(y * y * self.valid(i))
            normal, rate = norm_of(y)
            w.n_y[rows, :] = normal
            w.r_y[rows, :] = rate
            mid = w.h[rows, :].astype(F32) + (normal * self.row(SANDWICH_GAIN) + self.row(SANDWICH_BIAS))
            w.mid[rows, :] = mid
            normal, rate = norm_of(mid)
            w.n_m[rows, :] = normal
            w.r_m[rows, :] = rate
            w.c[rows, :] = (normal * self.row(SECOND_GAIN) + self.row(SECOND_BIAS)).astype(BF)

        self.chunks(middle)

    def fore_expand(self, block):
        w = self.w

        def body(tile):
            f = mxu(w.c[...], self.store[4 + block, :, tile], 1, 0)
            f = f + w.vec[EXPAND_BIAS + block : EXPAND_BIAS + block + 1, tile]
            square = f * f
            bent = jnp.tanh(CURVE * f * (1.0 + BEND * square))
            half = 0.5 * (1.0 + bent)
            w.g[block, :, tile] = (f * half).astype(BF)
            slope = half + 0.5 * f * (1.0 - bent * bent) * (CURVE * (1.0 + 3.0 * BEND * square))
            w.slope[block, :, tile] = slope.astype(BF)

        self.tiles(body)

    def fore_reduce(self):
        w = self.w

        def body(tile):
            e = mxu(w.g[0], self.store[8, :, tile], 1, 0)
            for block in range(1, 4):
                e = e + mxu(w.g[block], self.store[8 + block, :, tile], 1, 0)
            w.n_e[:, tile] = e + w.vec[REDUCE_BIAS : REDUCE_BIAS + 1, tile]

        self.tiles(body)

    def fore_end(self, target, first=0, last=None):
        w = self.w

        def body(rows, i):
            e = w.n_e[rows, :]
            valid = self.valid(i)
            w.sums[1:2, :] += column_sum(e * e * valid)
            normal, rate = norm_of(e)
            w.n_e[rows, :] = normal
            w.r_e[rows, :] = rate
            out = w.mid[rows, :] + (normal * self.row(CLOSING_GAIN) + self.row(CLOSING_BIAS))
            w.sums[2:3, :] += column_sum(out * out * valid)
            target[rows, :] = out.astype(BF)

        self.chunks(body, first, last)


    def back_start(self, seed, masked):
        w = self.w

        def body(rows, i):
            dout = seed[rows, :].astype(F32)
            if masked:
                dout = dout * self.valid(i)
            w.din[rows, :] = dout
            normal = w.n_e[rows, :]
            self.add(CLOSING_GAIN, column_sum(dout * normal))
            self.add(CLOSING_BIAS, column_sum(dout))
            de = norm_pull(dout, normal, w.r_e[rows, :], self.row(CLOSING_GAIN)).astype(BF)
            w.de[rows, :] = de
            self.add(REDUCE_BIAS, column_sum(de.astype(F32)))

        self.chunks(body)

    def back_reduce(self, block):
        w = self.w

        def body(tile):
            df = (mxu(w.de[...], self.store[8 + block, tile, :], 1, 1) * w.slope[block, :, tile].astype(F32)).astype(BF)
            w.slope[block, :, tile] = df
            w.dvec[EXPAND_BIAS + block : EXPAND_BIAS + block + 1, tile] = column_sum(df.astype(F32))

        self.tiles(body)

    def back_expand(self):
        w = self.w

        def body(tile):
            dc = mxu(w.slope[0], self.store[4, tile, :], 1, 1)
            for block in range(1, 4):
                dc = dc + mxu(w.slope[block], self.store[4 + block, tile, :], 1, 1)
            w.mid[:, tile] = dc

        self.tiles(body)

        def middle(rows, i):
            dc = w.mid[rows, :]
            normal = w.n_m[rows, :]
            self.add(SECOND_GAIN, column_sum(dc * normal))
            self.add(SECOND_BIAS, column_sum(dc))
            dmid = w.din[rows, :] + norm_pull(dc, normal, w.r_m[rows, :], self.row(SECOND_GAIN))
            w.din[rows, :] = dmid
            normal = w.n_y[rows, :]
            self.add(SANDWICH_GAIN, column_sum(dmid * normal))
            self.add(SANDWICH_BIAS, column_sum(dmid))
            dy = norm_pull(dmid, normal, w.r_y[rows, :], self.row(SANDWICH_GAIN)).astype(BF)
            w.dy[rows, :] = dy
            self.add(OUTPUT_BIAS, column_sum(dy.astype(F32)))

        self.chunks(middle)

    def back_output(self):
        w = self.w

        def body(tile):
            w.do[:, tile] = mxu(w.dy[...], self.store[3, tile, :], 1, 1).astype(BF)

        self.tiles(body)

    def back_attention(self):
        w, slots = self.w, self.slots

        def body(rows, lanes, i, length):
            grad = self.split(w.do[rows, lanes])
            probs = w.p[i]
            value = probs.astype(F32)
            dprobs = mxu(grad, w.v[rows, lanes], 1, 1)
            inner = jnp.sum(dprobs * value, axis=-1, keepdims=True)
            ds = (RELAX * value * (dprobs - inner)).astype(BF)
            wide = jnp.concatenate([ds[:slots], ds[slots:]], axis=1)
            dv = mxu(probs, grad, 0, 0)
            dk = mxu(ds, self.split(w.q[rows, lanes]), 0, 0)
            dq = mxu(wide, self.split(w.k[rows, lanes]), 1, 0) * QUERY_SCALE
            w.q[rows, lanes] = dq.astype(BF)
            w.k[rows, lanes] = dk.astype(BF)
            w.v[rows, lanes] = dv.astype(BF)

        self.pairs(body)

    def back_joint(self):
        w = self.w

        def body(tile):
            da = mxu(w.q[...], self.store[0, tile, :], 1, 1)
            da = da + mxu(w.k[...], self.store[1, tile, :], 1, 1)
            w.mid[:, tile] = da + mxu(w.v[...], self.store[2, tile, :], 1, 1)

        self.tiles(body)

    def back_end(self, target, first=0, last=None):
        w = self.w

        def body(rows, i):
            da = w.mid[rows, :]
            normal = w.n_h[rows, :]
            self.add(NORM_GAIN, column_sum(da * normal))
            self.add(NORM_BIAS, column_sum(da))
            self.add(QUERY_BIAS, column_sum(w.q[rows, :].astype(F32)))
            self.add(VALUE_BIAS, column_sum(w.v[rows, :].astype(F32)))
            din = w.din[rows, :] + norm_pull(da, normal, w.r_h[rows, :], self.row(NORM_GAIN))
            w.din[rows, :] = din
            target[rows, :] = din.astype(BF)

        self.chunks(body, first, last)


    def weight_grad(self, block):
        w = self.w
        if block < 3:
            left, right = w.a, (w.q, w.k, w.v)[block]
        elif block == 3:
            left, right = w.o, w.dy
        elif block < 8:
            left, right = w.c, w.slope.at[block - 4]
        else:
            left, right = w.g.at[block - 8], w.de

        def body(tile):
            self.store[block, tile, :] = mxu(left[:, tile], right[...], 0, 0).astype(BF)

        self.tiles(body)


def unfold_vectors(tiles, vec, count):
    for pair in range(count // 2):
        vec[:NARROW, pair * LANES : (pair + 1) * LANES] = tiles[2 * pair, :NARROW, :] + tiles[2 * pair + 1, :NARROW, :]
    half, quarter = count // 2, count // 4
    for shard in range(count):
        row, lane = QUERY_BIAS + shard // half, (shard % half) * LANES
        vec[row : row + 1, lane : lane + LANES] = tiles[shard, NARROW : NARROW + 1, :]
        for part in range(2):
            row, lane = EXPAND_BIAS + shard // quarter, ((shard % quarter) * 2 + part) * LANES
            source = NARROW + 1 + part
            vec[row : row + 1, lane : lane + LANES] = tiles[shard, source : source + 1, :]


def fold_vectors(tiles, dvec, figures, count):
    half, quarter = count // 2, count // 4
    for shard in range(count):
        pair = shard // 2
        tiles[shard, :NARROW, :] = dvec[:NARROW, pair * LANES : (pair + 1) * LANES]
        row, lane = QUERY_BIAS + shard // half, (shard % half) * LANES
        tiles[shard, NARROW : NARROW + 1, :] = dvec[row : row + 1, lane : lane + LANES]
        for part in range(2):
            row, lane = EXPAND_BIAS + shard // quarter, ((shard % quarter) * 2 + part) * LANES
            target = NARROW + 1 + part
            tiles[shard, target : target + 1, :] = dvec[row : row + 1, lane : lane + LANES]
        tiles[shard, FIGURES : FIGURES + 1, :] = figures
        tiles[shard, FIGURES + 1 :, :] = jnp.zeros((VECTOR_ROWS - FIGURES - 1, LANES), F32)


def figures_of(sums, lengths):
    lane = lax.broadcasted_iota(jnp.int32, (1, LANES), 1)
    row = jnp.zeros((1, LANES), F32)
    for i in range(3):
        row = jnp.where(lane == i, jnp.sum(sums[i : i + 1, :], axis=1, keepdims=True), row)
    seen = lengths[0]
    for i in range(1, lengths.shape[0]):
        seen = seen + lengths[i]
    return jnp.where(lane == 3, seen.astype(F32), row)


def relay_kernel(depth, lengths, tokens, cotangent, joint, output, expand, reduce, vectors,
                 section_out, section_grad, joint_out, output_out, expand_out, reduce_out, vector_out,
                 store, tiles, vec, dvec, sums, h, a, q, k, v, p, o, n_h, r_h, n_y, r_y, n_m, r_m, n_e, r_e,
                 mid, c, g, slope, de, dy, do, incoming, pass_sems, *rest):
    place = Place(depth)
    width = store.shape[2]
    count = 4 * depth
    gather_parts, rest = rest[:4], rest[4:]
    scatter_parts, vector_parts = rest[:12], rest[12:]
    work = Work(vec, dvec, h, a, q, k, v, p, o, n_h, r_h, n_y, r_y, n_m, r_m, n_e, r_e, mid, c, g, slope,
                de, dy, do, section_grad, sums)
    layer = Layer(work, store, lengths)
    slots = layer.slots
    first, second = place.s == 0, place.s == 1

    def passing(source, target, part, way):
        rows = pl.ds(part * slots, slots)
        return pltpu.make_async_remote_copy(
            source.at[rows], target.at[rows], pass_sems.at[way, 0, part], pass_sems.at[way, 1, part],
            device_id=place.across(), device_id_type=MESH)

    def forward(part):
        return passing(section_out, incoming, part, 0)

    def backward(part):
        return passing(do, incoming, part, 1)

    place.greet()
    dvec[...] = jnp.zeros_like(dvec)
    sums[...] = jnp.zeros_like(sums)

    def ready(item):
        if item == VECTOR_ITEM:
            unfold_vectors(tiles, vec, count)

        @pl.when(first)
        def _():
            if item == VECTOR_ITEM:
                layer.fore_start(tokens)
            elif item < 3:
                layer.fore_joint(item)
                if item == 2:
                    layer.fore_attention()
            elif item == 3:
                layer.fore_output()
            elif item < 8:
                layer.fore_expand(item - 4)
            elif item == BLOCKS - 1:
                layer.fore_reduce()
                for part in range(layer.sequences):
                    layer.fore_end(section_out, part * slots, (part + 1) * slots)
                    forward(part).start()

    gather = Gather(place, (joint, output, expand, reduce, vectors), store, tiles, gather_parts)
    run_gather(gather, ready)
    gather.drain()

    def chain(step):
        block = SCATTER_ORDER[step]
        if step == 0:
            for part in range(4):
                layer.back_reduce(part)
        elif step == 4:
            layer.back_expand()
        elif block == 3:
            layer.back_output()
        elif step == 9:
            layer.back_attention()
            layer.back_joint()

    @pl.when(second)
    def _():
        for part in range(layer.sequences):
            forward(part).wait_recv()
            layer.fore_start(incoming, part * slots, (part + 1) * slots)
        for block in range(3):
            layer.fore_joint(block)
        layer.fore_attention()
        layer.fore_output()
        for block in range(4):
            layer.fore_expand(block)
        layer.fore_reduce()
        layer.fore_end(section_out)
        layer.back_start(cotangent, True)
        for step in range(BLOCKS):
            chain(step)
        for part in range(layer.sequences):
            layer.back_end(do, part * slots, (part + 1) * slots)
            backward(part).start()

    @pl.when(first)
    def _():
        for part in range(layer.sequences):
            backward(part).wait_recv()
        layer.back_start(incoming, False)

    def fill(step):
        block = SCATTER_ORDER[step]

        @pl.when(first)
        def _():
            chain(step)
            if step == 9:
                layer.back_end(do)

        if step == 0:
            for part in range(4):
                layer.weight_grad(8 + part)
        elif step >= 4:
            layer.weight_grad(block)
        if step == BLOCKS - 1:
            fold_vectors(tiles, dvec, figures_of(sums, lengths), count)

    def part_of(step, shard):
        block, row = spot(SCATTER_ORDER[step], shard)
        return store.at[block, pl.ds(row, PART)]

    outs = [shard_view((joint_out, output_out, expand_out, reduce_out, vector_out), item, width) for item in SCATTER_ORDER]
    scatter = Scatter(place, part_of, BLOCKS, SLOTS, scatter_parts[:3], outs, scatter_parts[3:])
    vector_scatter = Scatter(place, lambda step, shard: tiles.at[shard], 1, 1, vector_parts[:3], [vector_out], vector_parts[3:])
    run_scatter(scatter, vector_scatter, fill)

    @pl.when(first)
    def _():
        for part in range(layer.sequences):
            forward(part).wait_send()

    @pl.when(second)
    def _():
        for part in range(layer.sequences):
            backward(part).wait_send()


def relay_local(depth, tokens, lengths, *parameters):
    cotangent, own = parameters[-1], Params(*parameters[:-1])
    micro, rows, width = tokens.shape
    sequences = lengths.shape[1] * micro
    count = micro * rows
    core = lax.axis_index("batch") % 2

    narrow = jnp.concatenate([
        own.norm_gain, own.norm_bias, own.output_bias, own.sandwich_gain, own.sandwich_bias, own.second_gain,
        own.second_bias, own.reduce_bias, own.closing_gain, own.closing_bias]).astype(F32)
    zero = jnp.zeros_like(narrow)
    narrow = jnp.where(core == 0, jnp.concatenate([narrow, zero], axis=1), jnp.concatenate([zero, narrow], axis=1))
    vectors = jnp.concatenate([
        narrow, own.joint_bias.astype(F32), own.expand_bias.astype(F32).reshape(2, LANES),
        jnp.zeros((VECTOR_ROWS - NARROW - 3, LANES), F32)])

    square = jax.ShapeDtypeStruct((count, width), F32)
    low, high, rate = (pltpu.VMEM((count, width), BF), pltpu.VMEM((count, width), F32), pltpu.VMEM((count, 1), F32))
    wide = pltpu.VMEM((4, count, width), BF)
    shards = 4 * depth
    dma = pltpu.SemaphoreType.DMA
    vmem, anywhere = pl.BlockSpec(memory_space=pltpu.VMEM), pl.BlockSpec(memory_space=pl.ANY)
    results = pl.pallas_call(
        functools.partial(relay_kernel, depth),
        out_shape=[
            jax.ShapeDtypeStruct((count, width), BF), square,
            jax.ShapeDtypeStruct((PART, 3 * width), F32), jax.ShapeDtypeStruct((PART, width), F32),
            jax.ShapeDtypeStruct((PART, 4 * width), F32), jax.ShapeDtypeStruct((4 * PART, width), F32),
            jax.ShapeDtypeStruct((VECTOR_ROWS, LANES), F32)],
        in_specs=[pl.BlockSpec(memory_space=pltpu.SMEM), vmem, vmem] + [anywhere] * 5,
        out_specs=[vmem] * 7,
        scratch_shapes=[
            pltpu.VMEM((BLOCKS, width, width), BF), pltpu.VMEM((shards, VECTOR_ROWS, LANES), F32),
            pltpu.VMEM((VECTOR_ROWS, width), F32), pltpu.VMEM((VECTOR_ROWS, width), F32), pltpu.VMEM((8, width), F32),
            low, low, low, low, low, pltpu.VMEM((sequences * width // LANES, 2 * rows // lengths.shape[1], rows // lengths.shape[1]), BF), low,
            high, rate, high, rate, high, rate, high, rate,
            high, low, wide, wide, low, low, low, low, dma((2, 2, sequences)),
        ] + gather_sems(depth) + scatter_scratch(depth, SLOTS, PART, width, BF) + scatter_scratch(depth, 1, VECTOR_ROWS, LANES, F32),
        compiler_params=pltpu.CompilerParams(collective_id=1, has_side_effects=True, vmem_limit_bytes=VMEM_LIMIT),
        cost_estimate=pl.CostEstimate(flops=6 * count * BLOCKS * width * width, bytes_accessed=2 * BLOCKS * width * width, transcendentals=0),
        name="relay",
    )(lengths.reshape(-1), tokens.reshape(count, width), cotangent.reshape(count, width),
      own.joint_weight[0], own.output_weight[0], own.expand_weight[0], own.reduce_weight[0], vectors)
    section_out, section_grad, joint, output, expand, reduce, tile = results

    halves = jnp.where(core == 0, tile[:NARROW, :HEAD_DIM], tile[:NARROW, HEAD_DIM:])
    narrow = [halves[i : i + 1] for i in range(NARROW)]
    figures = tile[FIGURES]
    magnitudes = jnp.sqrt(figures[:3] / (figures[3] * width))[None]
    grads = Params(
        norm_gain=narrow[NORM_GAIN], norm_bias=narrow[NORM_BIAS], joint_weight=joint[None],
        joint_bias=tile[NARROW : NARROW + 1], output_weight=output[None], output_bias=narrow[OUTPUT_BIAS],
        sandwich_gain=narrow[SANDWICH_GAIN], sandwich_bias=narrow[SANDWICH_BIAS], second_gain=narrow[SECOND_GAIN],
        second_bias=narrow[SECOND_BIAS], expand_weight=expand[None],
        expand_bias=tile[NARROW + 1 : NARROW + 3].reshape(1, -1), reduce_weight=reduce[None],
        reduce_bias=narrow[REDUCE_BIAS], closing_gain=narrow[CLOSING_GAIN], closing_bias=narrow[CLOSING_BIAS])
    shape = (1, micro, rows, width)
    return (section_out.reshape(shape), section_grad.reshape(shape), magnitudes) + tuple(grads)


def solution(mesh):
    vector, matrix = P("section", "batch"), P("section", "batch", None)
    kinds = tuple(matrix if i in MATRICES else vector for i in range(16))
    rows = P(None, "batch", None)
    stacked = P("section", None, "batch", None)
    devices = mesh.shape["batch"]
    body = functools.partial(relay_local, devices // 4) if devices == 16 else plain_local
    return jax.shard_map(
        body,
        mesh=mesh,
        in_specs=(rows, P(None, "batch")) + kinds + (rows,),
        out_specs=(stacked, stacked, P("section", None)) + kinds,
        check_vma=False,
    )
```

time: 887 us -> 455 us (0.51); the launches traced: 877 us -> 454 us
  waiting for transfers between devices: 618 us -> 0 us
  Pallas kernels: 0 us -> 436 us
  matrix products: 109 us -> 0 us
  blocking collectives: 53.4 us -> 0 us
  other arithmetic: 37.4 us -> 2.81 us
  local copies, waits for them, and re-layouts: 37.9 us -> 14.1 us
  between operations: 16.4 us -> 1.44 us
    pallas_call x0 -> x1, Pallas kernels: none -> 436 us  [relay_local(): pl.pallas_call(functools.partial(relay_kernel, depth), out_shape=[jax.Sha...]
    reduce_scatter x4 -> x0, waiting for transfers between devices: 361 us -> none  [local(): lax.psum_scatter(grads[name].astype(BF)[None], 'batch', scatter_dimension...]
    all_gather x4 -> x0, waiting for transfers between devices: 210 us -> none  [local(): w[name] = lax.all_gather(own[name], 'batch', axis=1, tiled=True)[0]]
    dot_general x28 -> x0, matrix products: 103 us -> none  [the longest x18 89.2 us: dot(): lax.dot_general(left, right, (contract, ((), ())), preferred_element_type...]
    psum x1 -> x0, blocking collectives: 30 us -> none  [local(): square_all, count_all = lax.psum((squares, count), 'batch')]
    ppermute x2 -> x0, waiting for transfers between devices: 25.4 us -> none  [passed_along(): return lax.ppermute(block, axis, route)]
    all_gather x1 -> x0, blocking collectives: 23.4 us -> none  [local(): packed = lax.all_gather(packed, 'batch', axis=0, tiled=True).astype(F32)]
    unnamed x10 -> x0, waiting for transfers between devices: 21.9 us -> none
  transfers between devices with their start and end apart: 11 -> 0, of which waited for: 11 -> 0; matrix products, arithmetic and copies ran while one was open for 8% -> 0% of each run, Pallas kernels for 0% -> 0%
where the time goes in v3:
time: 455 us; the launch traced here: 454 us
  Pallas kernels  436 us (96%)
  local copies, waits for them, and re-layouts  14.1 us (3%)
    pallas_call x1, Pallas kernels, relay_local(): pl.pallas_call(functools.partial(relay_kernel, depth), out_shape=[jax.Sha...  436 us
    unnamed x40, local copies, waits for them, and re-layouts  9.64 us

profile of v3, /device:TPU:0, one launch (start us, length us, event | category | flops | bytes accessed | tf_op | source)
XLA Modules:
  0.0 454.3 jit_solution(9355783691674784289)
XLA Ops:
  0.8 0.6 copy-done.13
  1.4 0.0 copy-done.9
  1.5 0.1 concatenate.12
  1.5 0.1 pad_select_fusion
  1.6 0.6 copy-done.5
  2.2 0.1 pad.5.clone
  2.3 0.6 copy-done.16
  2.9 0.7 maximum_maximum_fusion.vectors
  3.6 435.9 %relay.1 = (bf16[256,1024]{1,0:T(8,128)(2,1)}, f32[256,1024]{1,0:T(8,128)}, f32[64,3072]{1,0:T(8,128)}, f32[64,1024]{1,0:T(8,128)}, f32[64,4096]{1,0:T(8,128)}, /*index=5*/f32[256,1024]{1,0:T(8,128)}, f32[16,128]{1,0:T(8,128)}) custom-call(s32[2]{0:T(128)} %bitcast.30, bf16[256,1024]{1,0:T(8,128)(2,1)} %bitcast.24, bf16[256,1024]{1,0:T(8,128)(2,1)} %bitcast.25, ...), custom_call_target="tpu_custom_call" | custom-call | flops 19327352832 | bytes 25165824 | tf_op jit(solution)/shard_map/relay/pallas_call | solution.py:1162
  439.5 1.4 slice.54
  441.5 1.2 divide_sqrt_fusion
  442.7 0.8 slice_select_fusion
  443.5 0.6 fusion
  444.1 1.2 slice.65
  445.3 1.2 slice.59
  446.5 1.9 copy.44
  448.4 1.0 copy.45
  449.3 0.5 copy-done.3
  449.9 0.9 copy.46
  450.8 0.2 copy-done.4
  451.0 0.7 copy.47
  451.7 1.0 copy.48
  452.7 0.6 copy-done
  453.3 1.0 copy.49
  (31 shorter events, 0.2 us)
Async XLA Ops:
  0.7 0.7 copy-start.13
  0.7 0.7 copy-start.14
  0.7 0.7 copy-start.15
  0.7 0.7 copy-start.9
  0.7 0.7 copy-start.10
  0.7 0.7 copy-start.11
  0.7 0.7 copy-start.12
  0.7 0.7 copy-start.6
  0.8 0.7 copy-start.7
  0.8 0.7 copy-start.8
  1.5 0.7 copy-start.5
  2.2 0.7 copy-start.16
  439.4 8.9 %copy-start.2 = (f32[256,1024]{1,0:T(8,128)S(1)}, f32[256,1024]{1,0:T(8,128)}, u32[]{:S(2)}) copy-start(f32[256,1024]{1,0:T(8,128)} %get-tuple-element.27) | copy-start | bytes 3145732
  448.4 1.5 copy-start.3
  449.9 1.1 copy-start.4
  449.9 1.8 copy-start.1
  451.7 1.6 copy-start
